TPU v7x, 256 devices: a whole 4x4x8 slice. The times are simulated.
256 devices in a mesh: ex: 32 (over y_lo, z, core), feat: 8 (over y_hi, x).
Axes of the slice: x: 4, y: 4 (y_hi: 2, y_lo: 2; y = y_hi * 2 + y_lo), z: 8, core: 2. Of those that a mesh axis runs over, the one named last changes fastest.
Arguments:
- examples: bfloat16 [16384, 8192], P('ex', 'feat'), may hold values from -0.06591797 to 0.06591797
Outputs:
- bands: float32 [17, 16384, 512], P(None, ('ex', 'feat'))
All inputs are finite; a program needn't handle non-finite values.
Results may differ from a plain program's by a relative error of at most 0.0003.
Values may be sent and summed in bfloat16 or wider, within the bound.
No kernel may reach another device: no remote copies, remote signals or barrier semaphores. Data moves between devices by JAX's collectives and lax.ppermute only.
A program may use at most 128 MiB of HBM per device.

v0:
```python
import jax
import jax.numpy as jnp
from jax import lax
from jax.sharding import PartitionSpec as P


def shifted(value, axis, steps):
    count = lax.axis_size(axis)
    pairs = [(source, (source + steps) % count) for source in range(count)]
    return lax.ppermute(value, axis, pairs)


def per_device(examples):
    ex_count = lax.axis_size("ex")
    half_loop = ex_count // 2

    def product_with(other):
        return lax.dot_general(
            other, examples, (((1,), (1,)), ((), ())), preferred_element_type=jnp.float32
        )

    own_tile = product_with(examples)[None]

    def advance(carry, unused):
        arrived = shifted(carry, "ex", -1)
        return (arrived, product_with(arrived))

    unused_last, later = lax.scan(advance, examples, None, length=half_loop)
    partial_value = jnp.concatenate([own_tile, later], axis=0)
    return lax.psum_scatter(partial_value, "feat", scatter_dimension=1, tiled=True)


def solution(mesh):
    placed = (P("ex", "feat"),)
    return jax.shard_map(
        per_device,
        mesh=mesh,
        in_specs=placed,
        out_specs=P(None, ("ex", "feat"), None),
        check_vma=False,
    )
```

profile of v0, /device:TPU:1, one launch (start us, length us, event | category | flops | bytes accessed | tf_op | source)
XLA Modules:
  0.0 545.9 jit_solution(1714235250831954111)
XLA Ops:
  10.1 299.9 %while.12 = (s32[]{:T(128)}, bf16[512,1024]{1,0:T(8,128)(2,1)S(1)}, f32[16,512,512]{2,1,0:T(8,128)}, bf16[512,1024]{1,0:T(8,128)(2,1)}, s32[]{:T(128)}) while((s32[]{:T(128)}, bf16[512,1024]{1,0:T(8,128)(2,1)S(1)}, f32[16,512,512]{2,1,0:T(8,128)}, bf16[512,1024]{1,0:T(8,128)(2,1)}, s32[]{:T(128)}) %tuple.18), condition=%wide.region_1.2_spmd, body=%wide.region_0.1_spmd.sunk | while | flops 536870912 | bytes 9437297 | solution.py:28
  10.1 3.3 collective-permute-start
  13.4 12.3 %collective-permute-done = bf16[512,1024]{1,0:T(8,128)(2,1)S(1)} collective-permute-done((bf16[512,1024]{1,0:T(8,128)(2,1)S(1)}, bf16[512,1024]{1,0:T(8,128)(2,1)S(1)}, u32[]{:S(2)}, u32[]{:S(2)}) %collective-permute-start) | collective-permute-done | bytes 1048608 | tf_op jit(solution)/shard_map/while/body/eval_jaxpr/ppermute | solution.py:10
  28.8 4.6 collective-permute-start
  33.4 9.6 %collective-permute-done = bf16[512,1024]{1,0:T(8,128)(2,1)S(1)} collective-permute-done((bf16[512,1024]{1,0:T(8,128)(2,1)S(1)}, bf16[512,1024]{1,0:T(8,128)(2,1)S(1)}, u32[]{:S(2)}, u32[]{:S(2)}) %collective-permute-start) | collective-permute-done | bytes 1048608 | tf_op jit(solution)/shard_map/while/body/eval_jaxpr/ppermute | solution.py:10
  46.0 6.7 %collective-permute-start = (bf16[512,1024]{1,0:T(8,128)(2,1)S(1)}, bf16[512,1024]{1,0:T(8,128)(2,1)S(1)}, u32[]{:S(2)}, u32[]{:S(2)}) collective-permute-start(bf16[512,1024]{1,0:T(8,128)(2,1)S(1)} %get-tuple-element.67), channel_id=1, source_target_pairs={{0,248},{8,0},{16,8},{24,16},{32,24},{40,32},{48,40},{56,48},{64,5... | collective-permute-start | bytes 3145736 | tf_op jit(solution)/shard_map/while/body/eval_jaxpr/ppermute | solution.py:10
  52.8 7.5 %collective-permute-done = bf16[512,1024]{1,0:T(8,128)(2,1)S(1)} collective-permute-done((bf16[512,1024]{1,0:T(8,128)(2,1)S(1)}, bf16[512,1024]{1,0:T(8,128)(2,1)S(1)}, u32[]{:S(2)}, u32[]{:S(2)}) %collective-permute-start) | collective-permute-done | bytes 1048608 | tf_op jit(solution)/shard_map/while/body/eval_jaxpr/ppermute | solution.py:10
  63.3 8.8 %collective-permute-start = (bf16[512,1024]{1,0:T(8,128)(2,1)S(1)}, bf16[512,1024]{1,0:T(8,128)(2,1)S(1)}, u32[]{:S(2)}, u32[]{:S(2)}) collective-permute-start(bf16[512,1024]{1,0:T(8,128)(2,1)S(1)} %get-tuple-element.67), channel_id=1, source_target_pairs={{0,248},{8,0},{16,8},{24,16},{32,24},{40,32},{48,40},{56,48},{64,5... | collective-permute-start | bytes 3145736 | tf_op jit(solution)/shard_map/while/body/eval_jaxpr/ppermute | solution.py:10
  72.1 5.4 collective-permute-done
  80.5 10.9 %collective-permute-start = (bf16[512,1024]{1,0:T(8,128)(2,1)S(1)}, bf16[512,1024]{1,0:T(8,128)(2,1)S(1)}, u32[]{:S(2)}, u32[]{:S(2)}) collective-permute-start(bf16[512,1024]{1,0:T(8,128)(2,1)S(1)} %get-tuple-element.67), channel_id=1, source_target_pairs={{0,248},{8,0},{16,8},{24,16},{32,24},{40,32},{48,40},{56,48},{64,5... | collective-permute-start | bytes 3145736 | tf_op jit(solution)/shard_map/while/body/eval_jaxpr/ppermute | solution.py:10
  91.5 3.3 collective-permute-done
  97.8 13.0 %collective-permute-start = (bf16[512,1024]{1,0:T(8,128)(2,1)S(1)}, bf16[512,1024]{1,0:T(8,128)(2,1)S(1)}, u32[]{:S(2)}, u32[]{:S(2)}) collective-permute-start(bf16[512,1024]{1,0:T(8,128)(2,1)S(1)} %get-tuple-element.67), channel_id=1, source_target_pairs={{0,248},{8,0},{16,8},{24,16},{32,24},{40,32},{48,40},{56,48},{64,5... | collective-permute-start | bytes 3145736 | tf_op jit(solution)/shard_map/while/body/eval_jaxpr/ppermute | solution.py:10
  116.2 14.0 %collective-permute-start = (bf16[512,1024]{1,0:T(8,128)(2,1)S(1)}, bf16[512,1024]{1,0:T(8,128)(2,1)S(1)}, u32[]{:S(2)}, u32[]{:S(2)}) collective-permute-start(bf16[512,1024]{1,0:T(8,128)(2,1)S(1)} %get-tuple-element.67), channel_id=1, source_target_pairs={{0,248},{8,0},{16,8},{24,16},{32,24},{40,32},{48,40},{56,48},{64,5... | collective-permute-start | bytes 3145736 | tf_op jit(solution)/shard_map/while/body/eval_jaxpr/ppermute | solution.py:10
  135.5 14.0 %collective-permute-start = (bf16[512,1024]{1,0:T(8,128)(2,1)S(1)}, bf16[512,1024]{1,0:T(8,128)(2,1)S(1)}, u32[]{:S(2)}, u32[]{:S(2)}) collective-permute-start(bf16[512,1024]{1,0:T(8,128)(2,1)S(1)} %get-tuple-element.67), channel_id=1, source_target_pairs={{0,248},{8,0},{16,8},{24,16},{32,24},{40,32},{48,40},{56,48},{64,5... | collective-permute-start | bytes 3145736 | tf_op jit(solution)/shard_map/while/body/eval_jaxpr/ppermute | solution.py:10
  155.0 14.0 %collective-permute-start = (bf16[512,1024]{1,0:T(8,128)(2,1)S(1)}, bf16[512,1024]{1,0:T(8,128)(2,1)S(1)}, u32[]{:S(2)}, u32[]{:S(2)}) collective-permute-start(bf16[512,1024]{1,0:T(8,128)(2,1)S(1)} %get-tuple-element.67), channel_id=1, source_target_pairs={{0,248},{8,0},{16,8},{24,16},{32,24},{40,32},{48,40},{56,48},{64,5... | collective-permute-start | bytes 3145736 | tf_op jit(solution)/shard_map/while/body/eval_jaxpr/ppermute | solution.py:10
  174.3 14.0 %collective-permute-start = (bf16[512,1024]{1,0:T(8,128)(2,1)S(1)}, bf16[512,1024]{1,0:T(8,128)(2,1)S(1)}, u32[]{:S(2)}, u32[]{:S(2)}) collective-permute-start(bf16[512,1024]{1,0:T(8,128)(2,1)S(1)} %get-tuple-element.67), channel_id=1, source_target_pairs={{0,248},{8,0},{16,8},{24,16},{32,24},{40,32},{48,40},{56,48},{64,5... | collective-permute-start | bytes 3145736 | tf_op jit(solution)/shard_map/while/body/eval_jaxpr/ppermute | solution.py:10
  193.7 14.1 %collective-permute-start = (bf16[512,1024]{1,0:T(8,128)(2,1)S(1)}, bf16[512,1024]{1,0:T(8,128)(2,1)S(1)}, u32[]{:S(2)}, u32[]{:S(2)}) collective-permute-start(bf16[512,1024]{1,0:T(8,128)(2,1)S(1)} %get-tuple-element.67), channel_id=1, source_target_pairs={{0,248},{8,0},{16,8},{24,16},{32,24},{40,32},{48,40},{56,48},{64,5... | collective-permute-start | bytes 3145736 | tf_op jit(solution)/shard_map/while/body/eval_jaxpr/ppermute | solution.py:10
  213.0 14.0 %collective-permute-start = (bf16[512,1024]{1,0:T(8,128)(2,1)S(1)}, bf16[512,1024]{1,0:T(8,128)(2,1)S(1)}, u32[]{:S(2)}, u32[]{:S(2)}) collective-permute-start(bf16[512,1024]{1,0:T(8,128)(2,1)S(1)} %get-tuple-element.67), channel_id=1, source_target_pairs={{0,248},{8,0},{16,8},{24,16},{32,24},{40,32},{48,40},{56,48},{64,5... | collective-permute-start | bytes 3145736 | tf_op jit(solution)/shard_map/while/body/eval_jaxpr/ppermute | solution.py:10
  232.5 14.0 %collective-permute-start = (bf16[512,1024]{1,0:T(8,128)(2,1)S(1)}, bf16[512,1024]{1,0:T(8,128)(2,1)S(1)}, u32[]{:S(2)}, u32[]{:S(2)}) collective-permute-start(bf16[512,1024]{1,0:T(8,128)(2,1)S(1)} %get-tuple-element.67), channel_id=1, source_target_pairs={{0,248},{8,0},{16,8},{24,16},{32,24},{40,32},{48,40},{56,48},{64,5... | collective-permute-start | bytes 3145736 | tf_op jit(solution)/shard_map/while/body/eval_jaxpr/ppermute | solution.py:10
  251.8 14.0 %collective-permute-start = (bf16[512,1024]{1,0:T(8,128)(2,1)S(1)}, bf16[512,1024]{1,0:T(8,128)(2,1)S(1)}, u32[]{:S(2)}, u32[]{:S(2)}) collective-permute-start(bf16[512,1024]{1,0:T(8,128)(2,1)S(1)} %get-tuple-element.67), channel_id=1, source_target_pairs={{0,248},{8,0},{16,8},{24,16},{32,24},{40,32},{48,40},{56,48},{64,5... | collective-permute-start | bytes 3145736 | tf_op jit(solution)/shard_map/while/body/eval_jaxpr/ppermute | solution.py:10
  271.2 14.0 %collective-permute-start = (bf16[512,1024]{1,0:T(8,128)(2,1)S(1)}, bf16[512,1024]{1,0:T(8,128)(2,1)S(1)}, u32[]{:S(2)}, u32[]{:S(2)}) collective-permute-start(bf16[512,1024]{1,0:T(8,128)(2,1)S(1)} %get-tuple-element.67), channel_id=1, source_target_pairs={{0,248},{8,0},{16,8},{24,16},{32,24},{40,32},{48,40},{56,48},{64,5... | collective-permute-start | bytes 3145736 | tf_op jit(solution)/shard_map/while/body/eval_jaxpr/ppermute | solution.py:10
  290.6 14.0 %collective-permute-start = (bf16[512,1024]{1,0:T(8,128)(2,1)S(1)}, bf16[512,1024]{1,0:T(8,128)(2,1)S(1)}, u32[]{:S(2)}, u32[]{:S(2)}) collective-permute-start(bf16[512,1024]{1,0:T(8,128)(2,1)S(1)} %get-tuple-element.67), channel_id=1, source_target_pairs={{0,248},{8,0},{16,8},{24,16},{32,24},{40,32},{48,40},{56,48},{64,5... | collective-permute-start | bytes 3145736 | tf_op jit(solution)/shard_map/while/body/eval_jaxpr/ppermute | solution.py:10
  309.9 12.1 %pad_maximum_fusion = f32[17,512,512]{2,1,0:T(8,128)} fusion(f32[16,512,512]{2,1,0:T(8,128)} %get-tuple-element.27, f32[1,512,512]{2,1,0:T(8,128)S(1)} %convolution_bitcast_fusion.1), kind=kLoop, calls=%fused_computation.2 | loop fusion | flops 4456448 | bytes 35651584 | tf_op jit(solution)/shard_map/concatenate | solution.py:29
  322.0 217.0 %reduce-scatter.2.cloned.1.call-done = f32[17,64,512]{2,1,0:T(8,128)} async-done(((f32[17,512,512]{2,1,0:T(8,128)}), f32[17,64,512]{2,1,0:T(8,128)}) %reduce-scatter.2.cloned.1.call-update) | async-done | bytes 2228240 | tf_op jit(solution)/shard_map/reduce_scatter | solution.py:30
  (48 shorter events, 77.3 us)
Async XLA Ops:
  6.5 532.5 %reduce-scatter.2.cloned.1.call-start = ((), (), s32[]{:S(2)}) async-start(), calls=%async_computation.1 | async-start | bytes 20054016 | tf_op jit(solution)/shard_map/reduce_scatter | solution.py:30
  10.1 15.6 %collective-permute-start = (bf16[512,1024]{1,0:T(8,128)(2,1)S(1)}, bf16[512,1024]{1,0:T(8,128)(2,1)S(1)}, u32[]{:S(2)}, u32[]{:S(2)}) collective-permute-start(bf16[512,1024]{1,0:T(8,128)(2,1)S(1)} %get-tuple-element.67), channel_id=1, source_target_pairs={{0,248},{8,0},{16,8},{24,16},{32,24},{40,32},{48,40},{56,48},{64,5... | collective-permute-start | bytes 3145736 | tf_op jit(solution)/shard_map/while/body/eval_jaxpr/ppermute | solution.py:10
  28.8 14.2 %collective-permute-start = (bf16[512,1024]{1,0:T(8,128)(2,1)S(1)}, bf16[512,1024]{1,0:T(8,128)(2,1)S(1)}, u32[]{:S(2)}, u32[]{:S(2)}) collective-permute-start(bf16[512,1024]{1,0:T(8,128)(2,1)S(1)} %get-tuple-element.67), channel_id=1, source_target_pairs={{0,248},{8,0},{16,8},{24,16},{32,24},{40,32},{48,40},{56,48},{64,5... | collective-permute-start | bytes 3145736 | tf_op jit(solution)/shard_map/while/body/eval_jaxpr/ppermute | solution.py:10
  46.0 14.2 %collective-permute-start = (bf16[512,1024]{1,0:T(8,128)(2,1)S(1)}, bf16[512,1024]{1,0:T(8,128)(2,1)S(1)}, u32[]{:S(2)}, u32[]{:S(2)}) collective-permute-start(bf16[512,1024]{1,0:T(8,128)(2,1)S(1)} %get-tuple-element.67), channel_id=1, source_target_pairs={{0,248},{8,0},{16,8},{24,16},{32,24},{40,32},{48,40},{56,48},{64,5... | collective-permute-start | bytes 3145736 | tf_op jit(solution)/shard_map/while/body/eval_jaxpr/ppermute | solution.py:10
  63.3 14.2 %collective-permute-start = (bf16[512,1024]{1,0:T(8,128)(2,1)S(1)}, bf16[512,1024]{1,0:T(8,128)(2,1)S(1)}, u32[]{:S(2)}, u32[]{:S(2)}) collective-permute-start(bf16[512,1024]{1,0:T(8,128)(2,1)S(1)} %get-tuple-element.67), channel_id=1, source_target_pairs={{0,248},{8,0},{16,8},{24,16},{32,24},{40,32},{48,40},{56,48},{64,5... | collective-permute-start | bytes 3145736 | tf_op jit(solution)/shard_map/while/body/eval_jaxpr/ppermute | solution.py:10
  80.5 14.2 %collective-permute-start = (bf16[512,1024]{1,0:T(8,128)(2,1)S(1)}, bf16[512,1024]{1,0:T(8,128)(2,1)S(1)}, u32[]{:S(2)}, u32[]{:S(2)}) collective-permute-start(bf16[512,1024]{1,0:T(8,128)(2,1)S(1)} %get-tuple-element.67), channel_id=1, source_target_pairs={{0,248},{8,0},{16,8},{24,16},{32,24},{40,32},{48,40},{56,48},{64,5... | collective-permute-start | bytes 3145736 | tf_op jit(solution)/shard_map/while/body/eval_jaxpr/ppermute | solution.py:10
  97.8 15.3 %collective-permute-start = (bf16[512,1024]{1,0:T(8,128)(2,1)S(1)}, bf16[512,1024]{1,0:T(8,128)(2,1)S(1)}, u32[]{:S(2)}, u32[]{:S(2)}) collective-permute-start(bf16[512,1024]{1,0:T(8,128)(2,1)S(1)} %get-tuple-element.67), channel_id=1, source_target_pairs={{0,248},{8,0},{16,8},{24,16},{32,24},{40,32},{48,40},{56,48},{64,5... | collective-permute-start | bytes 3145736 | tf_op jit(solution)/shard_map/while/body/eval_jaxpr/ppermute | solution.py:10
  116.2 16.3 %collective-permute-start = (bf16[512,1024]{1,0:T(8,128)(2,1)S(1)}, bf16[512,1024]{1,0:T(8,128)(2,1)S(1)}, u32[]{:S(2)}, u32[]{:S(2)}) collective-permute-start(bf16[512,1024]{1,0:T(8,128)(2,1)S(1)} %get-tuple-element.67), channel_id=1, source_target_pairs={{0,248},{8,0},{16,8},{24,16},{32,24},{40,32},{48,40},{56,48},{64,5... | collective-permute-start | bytes 3145736 | tf_op jit(solution)/shard_map/while/body/eval_jaxpr/ppermute | solution.py:10
  135.5 16.3 %collective-permute-start = (bf16[512,1024]{1,0:T(8,128)(2,1)S(1)}, bf16[512,1024]{1,0:T(8,128)(2,1)S(1)}, u32[]{:S(2)}, u32[]{:S(2)}) collective-permute-start(bf16[512,1024]{1,0:T(8,128)(2,1)S(1)} %get-tuple-element.67), channel_id=1, source_target_pairs={{0,248},{8,0},{16,8},{24,16},{32,24},{40,32},{48,40},{56,48},{64,5... | collective-permute-start | bytes 3145736 | tf_op jit(solution)/shard_map/while/body/eval_jaxpr/ppermute | solution.py:10
  155.0 16.3 %collective-permute-start = (bf16[512,1024]{1,0:T(8,128)(2,1)S(1)}, bf16[512,1024]{1,0:T(8,128)(2,1)S(1)}, u32[]{:S(2)}, u32[]{:S(2)}) collective-permute-start(bf16[512,1024]{1,0:T(8,128)(2,1)S(1)} %get-tuple-element.67), channel_id=1, source_target_pairs={{0,248},{8,0},{16,8},{24,16},{32,24},{40,32},{48,40},{56,48},{64,5... | collective-permute-start | bytes 3145736 | tf_op jit(solution)/shard_map/while/body/eval_jaxpr/ppermute | solution.py:10
  174.3 16.3 %collective-permute-start = (bf16[512,1024]{1,0:T(8,128)(2,1)S(1)}, bf16[512,1024]{1,0:T(8,128)(2,1)S(1)}, u32[]{:S(2)}, u32[]{:S(2)}) collective-permute-start(bf16[512,1024]{1,0:T(8,128)(2,1)S(1)} %get-tuple-element.67), channel_id=1, source_target_pairs={{0,248},{8,0},{16,8},{24,16},{32,24},{40,32},{48,40},{56,48},{64,5... | collective-permute-start | bytes 3145736 | tf_op jit(solution)/shard_map/while/body/eval_jaxpr/ppermute | solution.py:10
  193.7 16.3 %collective-permute-start = (bf16[512,1024]{1,0:T(8,128)(2,1)S(1)}, bf16[512,1024]{1,0:T(8,128)(2,1)S(1)}, u32[]{:S(2)}, u32[]{:S(2)}) collective-permute-start(bf16[512,1024]{1,0:T(8,128)(2,1)S(1)} %get-tuple-element.67), channel_id=1, source_target_pairs={{0,248},{8,0},{16,8},{24,16},{32,24},{40,32},{48,40},{56,48},{64,5... | collective-permute-start | bytes 3145736 | tf_op jit(solution)/shard_map/while/body/eval_jaxpr/ppermute | solution.py:10
  213.0 16.3 %collective-permute-start = (bf16[512,1024]{1,0:T(8,128)(2,1)S(1)}, bf16[512,1024]{1,0:T(8,128)(2,1)S(1)}, u32[]{:S(2)}, u32[]{:S(2)}) collective-permute-start(bf16[512,1024]{1,0:T(8,128)(2,1)S(1)} %get-tuple-element.67), channel_id=1, source_target_pairs={{0,248},{8,0},{16,8},{24,16},{32,24},{40,32},{48,40},{56,48},{64,5... | collective-permute-start | bytes 3145736 | tf_op jit(solution)/shard_map/while/body/eval_jaxpr/ppermute | solution.py:10
  232.5 16.3 %collective-permute-start = (bf16[512,1024]{1,0:T(8,128)(2,1)S(1)}, bf16[512,1024]{1,0:T(8,128)(2,1)S(1)}, u32[]{:S(2)}, u32[]{:S(2)}) collective-permute-start(bf16[512,1024]{1,0:T(8,128)(2,1)S(1)} %get-tuple-element.67), channel_id=1, source_target_pairs={{0,248},{8,0},{16,8},{24,16},{32,24},{40,32},{48,40},{56,48},{64,5... | collective-permute-start | bytes 3145736 | tf_op jit(solution)/shard_map/while/body/eval_jaxpr/ppermute | solution.py:10
  251.8 16.3 %collective-permute-start = (bf16[512,1024]{1,0:T(8,128)(2,1)S(1)}, bf16[512,1024]{1,0:T(8,128)(2,1)S(1)}, u32[]{:S(2)}, u32[]{:S(2)}) collective-permute-start(bf16[512,1024]{1,0:T(8,128)(2,1)S(1)} %get-tuple-element.67), channel_id=1, source_target_pairs={{0,248},{8,0},{16,8},{24,16},{32,24},{40,32},{48,40},{56,48},{64,5... | collective-permute-start | bytes 3145736 | tf_op jit(solution)/shard_map/while/body/eval_jaxpr/ppermute | solution.py:10
  271.2 16.3 %collective-permute-start = (bf16[512,1024]{1,0:T(8,128)(2,1)S(1)}, bf16[512,1024]{1,0:T(8,128)(2,1)S(1)}, u32[]{:S(2)}, u32[]{:S(2)}) collective-permute-start(bf16[512,1024]{1,0:T(8,128)(2,1)S(1)} %get-tuple-element.67), channel_id=1, source_target_pairs={{0,248},{8,0},{16,8},{24,16},{32,24},{40,32},{48,40},{56,48},{64,5... | collective-permute-start | bytes 3145736 | tf_op jit(solution)/shard_map/while/body/eval_jaxpr/ppermute | solution.py:10
  290.6 16.3 %collective-permute-start = (bf16[512,1024]{1,0:T(8,128)(2,1)S(1)}, bf16[512,1024]{1,0:T(8,128)(2,1)S(1)}, u32[]{:S(2)}, u32[]{:S(2)}) collective-permute-start(bf16[512,1024]{1,0:T(8,128)(2,1)S(1)} %get-tuple-element.67), channel_id=1, source_target_pairs={{0,248},{8,0},{16,8},{24,16},{32,24},{40,32},{48,40},{56,48},{64,5... | collective-permute-start | bytes 3145736 | tf_op jit(solution)/shard_map/while/body/eval_jaxpr/ppermute | solution.py:10
Sparse Core Ops, SparseCore 0:
  322.2 216.8 reduce-scatter.1
where the time goes:
time: 548 us; the launch traced here: 546 us
  waiting for transfers between devices  280 us (51%)
  starting transfers between devices  188 us (34%)
  matrix products  49.8 us (9%)
  between operations  13.4 us (2%)
  other arithmetic  12.1 us (2%)
    reduce_scatter x1, waiting for transfers between devices, per_device(): lax.psum_scatter(partial_value, 'feat', scatter_dimension=1, tiled=True)  217 us
    ppermute x16, starting transfers between devices, shifted(): return lax.ppermute(value, axis, pairs)  188 us
    ppermute x16, waiting for transfers between devices, shifted(): return lax.ppermute(value, axis, pairs)  63.2 us
    dot_general x17, matrix products, product_with(): lax.dot_general(other, examples, (((1,), (1,)), ((), ())), preferred_elem...  49.8 us
    concatenate x1, other arithmetic, per_device(): partial_value = jnp.concatenate([own_tile, later], axis=0)  12.1 us
  transfers between devices with their start and end apart: 17, of which 17 were waited for; matrix products, arithmetic and copies ran while one was open for 0% of the time, Pallas kernels for 0%

commit v1 on v0

v1 whole, which is shorter than its diff:
```python
import jax
import jax.numpy as jnp
from jax import lax
from jax.experimental import pallas as pl
from jax.experimental.pallas import tpu as pltpu
from jax.sharding import PartitionSpec as P


def tiles_kernel(full_ref, *refs):
    slice_refs, out_ref = refs[:-1], refs[-1]
    rows = jnp.concatenate([ref[0] for ref in slice_refs], axis=0)
    product = lax.dot_general(
        rows, full_ref[0], (((1,), (1,)), ((), ())), preferred_element_type=jnp.float32
    )
    product = product.reshape(out_ref.shape)

    @pl.when(pl.program_id(0) == 0)
    def _():
        out_ref[...] = product

    @pl.when(pl.program_id(0) > 0)
    def _():
        out_ref[...] += product


def tiles(full, slices):
    parts, wide, depth = full.shape
    rows = slices[0].shape[1]
    count = len(slices)
    return pl.pallas_call(
        tiles_kernel,
        grid=(parts,),
        in_specs=[pl.BlockSpec((1, wide, depth), lambda f: (f, 0, 0))]
        + [pl.BlockSpec((1, rows, depth), lambda f: (f, 0, 0))] * count,
        out_specs=pl.BlockSpec((count, rows, wide), lambda f: (0, 0, 0)),
        out_shape=jax.ShapeDtypeStruct((count, rows, wide), jnp.float32),
        compiler_params=pltpu.CompilerParams(vmem_limit_bytes=24 * 1024 * 1024),
        cost_estimate=pl.CostEstimate(
            flops=2 * parts * wide * depth * rows * count,
            bytes_accessed=2 * parts * depth * (wide + rows * count) + 4 * count * rows * wide,
            transcendentals=0,
        ),
    )(full, *slices)


def per_device(examples):
    blocks = lax.axis_size("ex")
    feats = lax.axis_size("feat")
    half = blocks // 2
    steps = blocks // 8
    core = lax.axis_index("ex") % 2
    rows, depth = examples.shape

    full = lax.all_gather(examples, "feat", axis=0)
    own = lax.all_to_all(examples.reshape(feats, rows // feats, depth), "feat", 0, 0)

    swap_pairs = [(i, i ^ 1) for i in range(blocks)]
    first_pairs = [(i, (i - 2) % blocks if i % 2 == 0 else (i + half) % blocks) for i in range(blocks)]
    later_pairs = [(i, (i - 2) % blocks if i % 2 == 0 else (i + 2) % blocks) for i in range(blocks)]

    other = lax.ppermute(own, "ex", swap_pairs)
    found = tiles(full, [own, other])
    even = jnp.where(core == 0, found[0], found[1])
    odd = jnp.where(core == 0, found[1], found[0])
    table = [None] * (half + 2)
    table[0], table[1] = even, odd
    held = [own, other]
    for step in range(1, steps + 1):
        pairs = first_pairs if step == 1 else later_pairs
        held = [lax.ppermute(piece, "ex", pairs) for piece in held]
        across = [lax.ppermute(piece, "ex", swap_pairs) for piece in held]
        found = tiles(full, held + across)
        low, high = step, half // 2 + 1 - step
        table[2 * low] = jnp.where(core == 0, found[0], found[2])
        table[2 * low + 1] = jnp.where(core == 0, found[1], found[3])
        table[2 * high + 1] = jnp.where(core == 0, found[2], found[0])
        table[2 * high] = jnp.where(core == 0, found[3], found[1])
    return jnp.where(core == 0, jnp.stack(table[:-1]), jnp.stack(table[1:]))


def solution(mesh):
    placed = (P("ex", "feat"),)
    return jax.shard_map(
        per_device,
        mesh=mesh,
        in_specs=placed,
        out_specs=P(None, ("ex", "feat"), None),
        check_vma=False,
    )
```

time: 548 us -> 305 us (0.56)
  starting transfers between devices: 188 us -> 8.27 us
  waiting for transfers between devices: 280 us -> 218 us
  matrix products: 49.8 us -> 0 us
  Pallas kernels: 0 us -> 30.3 us
  blocking collectives: 0 us -> 23.8 us
  other arithmetic: 12.1 us -> 2.64 us
    reduce_scatter x1 -> x0, waiting for transfers between devices: 217 us -> none  [per_device(): lax.psum_scatter(partial_value, 'feat', scatter_dimension=1, tiled=True)]
    ppermute x16 -> x17, starting transfers between devices: 188 us -> 8.27 us  [the longest x8 4.09 us: per_device(): held = [lax.ppermute(piece, 'ex', pairs) for piece in held]]
    all_gather x0 -> x1, waiting for transfers between devices: none -> 82.9 us  [per_device(): full = lax.all_gather(examples, 'feat', axis=0)]
    ppermute x16 -> x17, waiting for transfers between devices: 63.2 us -> 135 us  [the longest x8 133 us: per_device(): held = [lax.ppermute(piece, 'ex', pairs) for piece in held]]
    dot_general x17 -> x0, matrix products: 49.8 us -> none  [product_with(): lax.dot_general(other, examples, (((1,), (1,)), ((), ())), preferred_elem...]
    pallas_call x0 -> x5, Pallas kernels: none -> 30.3 us  [tiles(): pl.pallas_call(tiles_kernel, grid=(parts,), in_specs=[pl.BlockSpec((1, wi...]
    all_to_all x0 -> x1, blocking collectives: none -> 23.8 us  [per_device(): lax.all_to_all(examples.reshape(feats, rows // feats, depth), 'feat', 0, 0)]
    concatenate x1 -> x0, other arithmetic: 12.1 us -> none  [per_device(): partial_value = jnp.concatenate([own_tile, later], axis=0)]
  transfers between devices with their start and end apart: 17 -> 18, of which waited for: 17 -> 8; matrix products, arithmetic and copies ran while one was open for 0% -> 0% of each run, Pallas kernels for 0% -> 8%
where the time goes in v1:
time: 305 us
  waiting for transfers between devices  218 us (71%)
  Pallas kernels  30.3 us (10%)
  blocking collectives  23.8 us (8%)
  between operations  13.7 us (4%)
  starting transfers between devices  8.27 us (3%)
  local copies, waits for them, and re-layouts  7.52 us (2%)
    ppermute x8, waiting for transfers between devices, per_device(): held = [lax.ppermute(piece, 'ex', pairs) for piece in held]  133 us
    all_gather x1, waiting for transfers between devices, per_device(): full = lax.all_gather(examples, 'feat', axis=0)  82.9 us
    pallas_call x5, Pallas kernels, tiles(): pl.pallas_call(tiles_kernel, grid=(parts,), in_specs=[pl.BlockSpec((1, wi...  30.3 us
    all_to_all x1, blocking collectives, per_device(): lax.all_to_all(examples.reshape(feats, rows // feats, depth), 'feat', 0, 0)  23.8 us
    unnamed x14, local copies, waits for them, and re-layouts  7.52 us
  transfers between devices with their start and end apart: 18, of which 8 were waited for; matrix products, arithmetic and copies ran while one was open for 0% of the time, Pallas kernels for 8%

profile of v1, /device:TPU:1, one launch (start us, length us, event | category | flops | bytes accessed | tf_op | source)
XLA Modules:
  0.0 304.6 jit_solution(17810734343845130711)
XLA Ops:
  7.3 23.8 %all_to_all.5.refs_0_ = bf16[8,64,1024]{2,1,0:T(8,128)(2,1)S(1)} all-to-all(bf16[8,64,1024]{2,1,0:T(8,128)(2,1)} %bitcast.7), channel_id=1, replica_groups=mesh['ex'=32,'feat'=8] {'feat'}, dimensions={0} | all-to-all | bytes 2097152 | tf_op jit(solution)/shard_map/all_to_all | solution.py:55
  31.0 1.9 collective-permute-start
  33.3 1.9 collective-permute-done.refs_1_
  35.6 1.0 copy-done.5
  36.6 16.2 %collective-permute-done.1.refs_0_ = bf16[8,64,1024]{2,1,0:T(8,128)(2,1)S(1)} collective-permute-done((bf16[8,64,1024]{2,1,0:T(8,128)(2,1)S(1)}, bf16[8,64,1024]{2,1,0:T(8,128)(2,1)S(1)}, u32[]{:S(2)}, u32[]{:S(2)}) %collective-permute-start.1) | collective-permute-done | bytes 1048608 | tf_op jit(solution)/shard_map/ppermute | solution.py:70
  52.8 1.6 collective-permute-start.5
  54.4 9.5 %collective-permute-done.2.refs_1_ = bf16[8,64,1024]{2,1,0:T(8,128)(2,1)} collective-permute-done((bf16[8,64,1024]{2,1,0:T(8,128)(2,1)S(1)}, bf16[8,64,1024]{2,1,0:T(8,128)(2,1)}, u32[]{:S(2)}, u32[]{:S(2)}) %collective-permute-start.2) | collective-permute-done | bytes 1048608 | tf_op jit(solution)/shard_map/ppermute | solution.py:70
  63.9 1.6 collective-permute-start.6
  65.6 72.7 %collective-permute-done.5.refs_0_ = bf16[8,64,1024]{2,1,0:T(8,128)(2,1)S(1)} collective-permute-done((bf16[8,64,1024]{2,1,0:T(8,128)(2,1)S(1)}, bf16[8,64,1024]{2,1,0:T(8,128)(2,1)S(1)}, u32[]{:S(2)}, u32[]{:S(2)}) %collective-permute-start.5) | collective-permute-done | bytes 1048608 | tf_op jit(solution)/shard_map/ppermute | solution.py:70
  138.3 13.4 %collective-permute-done.6.refs_1_ = bf16[8,64,1024]{2,1,0:T(8,128)(2,1)} collective-permute-done((bf16[8,64,1024]{2,1,0:T(8,128)(2,1)}, bf16[8,64,1024]{2,1,0:T(8,128)(2,1)}, u32[]{:S(2)}, u32[]{:S(2)}) %collective-permute-start.6) | collective-permute-done | bytes 1048608 | tf_op jit(solution)/shard_map/ppermute | solution.py:70
  151.7 1.0 copy-done.1
  153.2 9.7 %collective-permute-done.9.refs_0_ = bf16[8,64,1024]{2,1,0:T(8,128)(2,1)S(1)} collective-permute-done((bf16[8,64,1024]{2,1,0:T(8,128)(2,1)S(1)}, bf16[8,64,1024]{2,1,0:T(8,128)(2,1)S(1)}, u32[]{:S(2)}, u32[]{:S(2)}) %collective-permute-start.9) | collective-permute-done | bytes 1048608 | tf_op jit(solution)/shard_map/ppermute | solution.py:70
  163.0 11.2 %collective-permute-done.10.refs_1_ = bf16[8,64,1024]{2,1,0:T(8,128)(2,1)} collective-permute-done((bf16[8,64,1024]{2,1,0:T(8,128)(2,1)}, bf16[8,64,1024]{2,1,0:T(8,128)(2,1)}, u32[]{:S(2)}, u32[]{:S(2)}) %collective-permute-start.10) | collective-permute-done | bytes 1048608 | tf_op jit(solution)/shard_map/ppermute | solution.py:70
  174.2 1.0 copy-done.3
  175.2 82.9 %all-gather.3.cloned.1.call-done = bf16[4096,1024]{1,0:T(8,128)(2,1)} async-done(((bf16[512,1024]{1,0:T(8,128)(2,1)}), bf16[4096,1024]{1,0:T(8,128)(2,1)}) %all-gather.3.cloned.1.call-update) | async-done | bytes 8388624 | tf_op jit(solution)/shard_map/all_gather | solution.py:54
  258.0 3.4 %copy-done = bf16[4096,1024]{1,0:T(8,128)(2,1)S(1)} copy-done((bf16[4096,1024]{1,0:T(8,128)(2,1)S(1)}, bf16[4096,1024]{1,0:T(8,128)(2,1)}, u32[]{:S(2)}) %copy-start) | copy-done | bytes 8388632
  261.4 1.2 copy-done.6
  262.6 4.1 %shard_map.17 = f32[2,64,512]{2,1,0:T(8,128)S(1)} custom-call(bf16[8,512,1024]{2,1,0:T(8,128)(2,1)S(1)} %bitcast.2, bf16[8,64,1024]{2,1,0:T(8,128)(2,1)S(1)} %all_to_all.5.refs_0_, bf16[8,64,1024]{2,1,0:T(8,128)(2,1)S(1)} %copy-done.6), custom_call_target="tpu_custom_call" | custom-call | flops 1073741824 | bytes 10747904 | tf_op jit(solution)/shard_map/pallas_call | solution.py:30
  266.7 0.9 collective-permute-start.11
  267.8 6.6 %shard_map.18 = f32[4,64,512]{2,1,0:T(8,128)S(1)} custom-call(bf16[8,512,1024]{2,1,0:T(8,128)(2,1)S(1)} %bitcast.3, bf16[8,64,1024]{2,1,0:T(8,128)(2,1)S(1)} %copy-done.2, bf16[8,64,1024]{2,1,0:T(8,128)(2,1)} %collective-permute-done.2.refs_1_, bf16[8,64,1024]{2,1,0:T(8,128)(2,1)S(1)} %copy-done.4, bf16[8,64,1024]{2,1,0:T(8,128)(2,1)} %collective-permute-done.4.refs_3_), custom_call_target="tpu_custom_call" | custom-call | flops 2147483648 | bytes 13107200 | tf_op jit(solution)/shard_map/pallas_call | solution.py:30
  275.1 6.8 %shard_map.19 = f32[4,64,512]{2,1,0:T(8,128)S(1)} custom-call(bf16[8,512,1024]{2,1,0:T(8,128)(2,1)S(1)} %bitcast.4, bf16[8,64,1024]{2,1,0:T(8,128)(2,1)S(1)} %collective-permute-done.5.refs_0_, bf16[8,64,1024]{2,1,0:T(8,128)(2,1)} %collective-permute-done.6.refs_1_, bf16[8,64,1024]{2,1,0:T(8,128)(2,1)} %collective-permute-done.7.refs_2_, ...), custom_call_target="tpu_custom_call" | custom-call | flops 2147483648 | bytes 13107200 | tf_op jit(solution)/shard_map/pallas_call | solution.py:30
  282.0 6.3 %shard_map.20 = f32[4,64,512]{2,1,0:T(8,128)S(1)} custom-call(bf16[8,512,1024]{2,1,0:T(8,128)(2,1)S(1)} %bitcast.5, bf16[8,64,1024]{2,1,0:T(8,128)(2,1)S(1)} %collective-permute-done.9.refs_0_, bf16[8,64,1024]{2,1,0:T(8,128)(2,1)} %collective-permute-done.10.refs_1_, bf16[8,64,1024]{2,1,0:T(8,128)(2,1)S(1)} %collective-permute-done.11.refs_2_, ...), custom_call_target="tpu_custom_call" | custom-call | flops 2147483648 | bytes 13107200 | tf_op jit(solution)/shard_map/pallas_call | solution.py:30
  288.4 6.6 %shard_map.21 = f32[4,64,512]{2,1,0:T(8,128)S(1)} custom-call(bf16[8,512,1024]{2,1,0:T(8,128)(2,1)S(1)} %bitcast.6, bf16[8,64,1024]{2,1,0:T(8,128)(2,1)} %collective-permute-done.13.refs_0_, bf16[8,64,1024]{2,1,0:T(8,128)(2,1)} %collective-permute-done.14.refs_1_, bf16[8,64,1024]{2,1,0:T(8,128)(2,1)S(1)} %collective-permute-done.15.refs_2_, ...), custom_call_target="tpu_custom_call" | custom-call | flops 2147483648 | bytes 13107200 | tf_op jit(solution)/shard_map/pallas_call | solution.py:30
  295.7 2.0 broadcast_select_fusion
  (65 shorter events, 3.6 us)
Async XLA Ops:
  6.5 251.5 %all-gather.3.cloned.1.call-start = ((), (), s32[]{:S(2)}) async-start(), calls=%async_computation.1 | async-start | bytes 9437184 | tf_op jit(solution)/shard_map/all_gather | solution.py:54
  31.0 4.2 %collective-permute-start = (bf16[8,64,1024]{2,1,0:T(8,128)(2,1)S(1)}, bf16[8,64,1024]{2,1,0:T(8,128)(2,1)S(1)}, u32[]{:S(2)}, u32[]{:S(2)}) collective-permute-start(bf16[8,64,1024]{2,1,0:T(8,128)(2,1)S(1)} %all_to_all.5.refs_0_), channel_id=1, source_target_pairs={{0,8},{8,0},{16,24},{24,16},{32,40},{40,32},{48,56},{56,48},{64,72... | collective-permute-start | bytes 3145736 | tf_op jit(solution)/shard_map/ppermute | solution.py:61
  32.9 19.9 %collective-permute-start.1 = (bf16[8,64,1024]{2,1,0:T(8,128)(2,1)S(1)}, bf16[8,64,1024]{2,1,0:T(8,128)(2,1)S(1)}, u32[]{:S(2)}, u32[]{:S(2)}) collective-permute-start(bf16[8,64,1024]{2,1,0:T(8,128)(2,1)S(1)} %all_to_all.5.refs_0_), channel_id=1, source_target_pairs={{0,240},{8,136},{16,0},{24,152},{32,16},{40,168},{48,32},{56,184},... | collective-permute-start | bytes 3145736 | tf_op jit(solution)/shard_map/ppermute | solution.py:70
  35.2 28.7 %collective-permute-start.2 = (bf16[8,64,1024]{2,1,0:T(8,128)(2,1)S(1)}, bf16[8,64,1024]{2,1,0:T(8,128)(2,1)}, u32[]{:S(2)}, u32[]{:S(2)}) collective-permute-start(bf16[8,64,1024]{2,1,0:T(8,128)(2,1)S(1)} %collective-permute-done.refs_1_), channel_id=1, source_target_pairs={{0,240},{8,136},{16,0},{24,152},{32,16},{40,168},{48,32},{56,184},... | collective-permute-start | bytes 3145736 | tf_op jit(solution)/shard_map/ppermute | solution.py:70
  35.6 1.0 copy-start.5
  52.8 85.5 %collective-permute-start.5 = (bf16[8,64,1024]{2,1,0:T(8,128)(2,1)S(1)}, bf16[8,64,1024]{2,1,0:T(8,128)(2,1)S(1)}, u32[]{:S(2)}, u32[]{:S(2)}) collective-permute-start(bf16[8,64,1024]{2,1,0:T(8,128)(2,1)S(1)} %collective-permute-done.1.refs_0_), channel_id=1, source_target_pairs={{0,240},{8,24},{16,0},{24,40},{32,16},{40,56},{48,32},{56,72},{64,... | collective-permute-start | bytes 3145736 | tf_op jit(solution)/shard_map/ppermute | solution.py:70
  63.9 87.8 %collective-permute-start.6 = (bf16[8,64,1024]{2,1,0:T(8,128)(2,1)}, bf16[8,64,1024]{2,1,0:T(8,128)(2,1)}, u32[]{:S(2)}, u32[]{:S(2)}) collective-permute-start(bf16[8,64,1024]{2,1,0:T(8,128)(2,1)} %collective-permute-done.2.refs_1_), channel_id=1, source_target_pairs={{0,240},{8,24},{16,0},{24,40},{32,16},{40,56},{48,32},{56,72},{64,... | collective-permute-start | bytes 3145736 | tf_op jit(solution)/shard_map/ppermute | solution.py:70
  138.3 24.6 %collective-permute-start.9 = (bf16[8,64,1024]{2,1,0:T(8,128)(2,1)S(1)}, bf16[8,64,1024]{2,1,0:T(8,128)(2,1)S(1)}, u32[]{:S(2)}, u32[]{:S(2)}) collective-permute-start(bf16[8,64,1024]{2,1,0:T(8,128)(2,1)S(1)} %collective-permute-done.5.refs_0_), channel_id=1, source_target_pairs={{0,240},{8,24},{16,0},{24,40},{32,16},{40,56},{48,32},{56,72},{64,... | collective-permute-start | bytes 3145736 | tf_op jit(solution)/shard_map/ppermute | solution.py:70
  151.7 22.5 %collective-permute-start.10 = (bf16[8,64,1024]{2,1,0:T(8,128)(2,1)}, bf16[8,64,1024]{2,1,0:T(8,128)(2,1)}, u32[]{:S(2)}, u32[]{:S(2)}) collective-permute-start(bf16[8,64,1024]{2,1,0:T(8,128)(2,1)} %collective-permute-done.6.refs_1_), channel_id=1, source_target_pairs={{0,240},{8,24},{16,0},{24,40},{32,16},{40,56},{48,32},{56,72},{64,... | collective-permute-start | bytes 3145736 | tf_op jit(solution)/shard_map/ppermute | solution.py:70
  151.7 22.5 %collective-permute-start.3 = (bf16[8,64,1024]{2,1,0:T(8,128)(2,1)S(1)}, bf16[8,64,1024]{2,1,0:T(8,128)(2,1)S(1)}, u32[]{:S(2)}, u32[]{:S(2)}) collective-permute-start(bf16[8,64,1024]{2,1,0:T(8,128)(2,1)S(1)} %collective-permute-done.1.refs_0_), channel_id=1, source_target_pairs={{0,8},{8,0},{16,24},{24,16},{32,40},{40,32},{48,56},{56,48},{64,72... | collective-permute-start | bytes 3145736 | tf_op jit(solution)/shard_map/ppermute | solution.py:71
  151.7 1.0 copy-start.1
  152.7 114.0 %collective-permute-start.4 = (bf16[8,64,1024]{2,1,0:T(8,128)(2,1)}, bf16[8,64,1024]{2,1,0:T(8,128)(2,1)}, u32[]{:S(2)}, u32[]{:S(2)}) collective-permute-start(bf16[8,64,1024]{2,1,0:T(8,128)(2,1)} %collective-permute-done.2.refs_1_), channel_id=1, source_target_pairs={{0,8},{8,0},{16,24},{24,16},{32,40},{40,32},{48,56},{56,48},{64,72... | collective-permute-start | bytes 3145736 | tf_op jit(solution)/shard_map/ppermute | solution.py:71
  153.2 114.4 %collective-permute-start.7 = (bf16[8,64,1024]{2,1,0:T(8,128)(2,1)S(1)}, bf16[8,64,1024]{2,1,0:T(8,128)(2,1)}, u32[]{:S(2)}, u32[]{:S(2)}) collective-permute-start(bf16[8,64,1024]{2,1,0:T(8,128)(2,1)S(1)} %collective-permute-done.5.refs_0_), channel_id=1, source_target_pairs={{0,8},{8,0},{16,24},{24,16},{32,40},{40,32},{48,56},{56,48},{64,72... | collective-permute-start | bytes 3145736 | tf_op jit(solution)/shard_map/ppermute | solution.py:71
  162.9 111.4 %collective-permute-start.13 = (bf16[8,64,1024]{2,1,0:T(8,128)(2,1)S(1)}, bf16[8,64,1024]{2,1,0:T(8,128)(2,1)}, u32[]{:S(2)}, u32[]{:S(2)}) collective-permute-start(bf16[8,64,1024]{2,1,0:T(8,128)(2,1)S(1)} %collective-permute-done.9.refs_0_), channel_id=1, source_target_pairs={{0,240},{8,24},{16,0},{24,40},{32,16},{40,56},{48,32},{56,72},{64,... | collective-permute-start | bytes 3145736 | tf_op jit(solution)/shard_map/ppermute | solution.py:70
  174.2 100.6 %collective-permute-start.14 = (bf16[8,64,1024]{2,1,0:T(8,128)(2,1)}, bf16[8,64,1024]{2,1,0:T(8,128)(2,1)}, u32[]{:S(2)}, u32[]{:S(2)}) collective-permute-start(bf16[8,64,1024]{2,1,0:T(8,128)(2,1)} %collective-permute-done.10.refs_1_), channel_id=1, source_target_pairs={{0,240},{8,24},{16,0},{24,40},{32,16},{40,56},{48,32},{56,72},{64,... | collective-permute-start | bytes 3145736 | tf_op jit(solution)/shard_map/ppermute | solution.py:70
  175.2 100.0 %collective-permute-start.8 = (bf16[8,64,1024]{2,1,0:T(8,128)(2,1)}, bf16[8,64,1024]{2,1,0:T(8,128)(2,1)}, u32[]{:S(2)}, u32[]{:S(2)}) collective-permute-start(bf16[8,64,1024]{2,1,0:T(8,128)(2,1)} %collective-permute-done.6.refs_1_), channel_id=1, source_target_pairs={{0,8},{8,0},{16,24},{24,16},{32,40},{40,32},{48,56},{56,48},{64,72... | collective-permute-start | bytes 3145736 | tf_op jit(solution)/shard_map/ppermute | solution.py:71
  258.0 3.4 %copy-start = (bf16[4096,1024]{1,0:T(8,128)(2,1)S(1)}, bf16[4096,1024]{1,0:T(8,128)(2,1)}, u32[]{:S(2)}) copy-start(bf16[4096,1024]{1,0:T(8,128)(2,1)} %all-gather.3.cloned.1.call-done) | copy-start | bytes 25165828
  261.4 1.2 copy-start.6
  262.6 5.1 %copy-start.2 = (bf16[8,64,1024]{2,1,0:T(8,128)(2,1)S(1)}, bf16[8,64,1024]{2,1,0:T(8,128)(2,1)}, u32[]{:S(2)}) copy-start(bf16[8,64,1024]{2,1,0:T(8,128)(2,1)} %copy-done.1) | copy-start | bytes 3145732
  262.6 5.1 %copy-start.4 = (bf16[8,64,1024]{2,1,0:T(8,128)(2,1)S(1)}, bf16[8,64,1024]{2,1,0:T(8,128)(2,1)}, u32[]{:S(2)}) copy-start(bf16[8,64,1024]{2,1,0:T(8,128)(2,1)} %copy-done.3) | copy-start | bytes 3145732
  266.7 15.3 %collective-permute-start.11 = (bf16[8,64,1024]{2,1,0:T(8,128)(2,1)S(1)}, bf16[8,64,1024]{2,1,0:T(8,128)(2,1)S(1)}, u32[]{:S(2)}, u32[]{:S(2)}) collective-permute-start(bf16[8,64,1024]{2,1,0:T(8,128)(2,1)S(1)} %collective-permute-done.9.refs_0_), channel_id=1, source_target_pairs={{0,8},{8,0},{16,24},{24,16},{32,40},{40,32},{48,56},{56,48},{64,72... | collective-permute-start | bytes 3145736 | tf_op jit(solution)/shard_map/ppermute | solution.py:71
  267.6 14.4 %collective-permute-start.12 = (bf16[8,64,1024]{2,1,0:T(8,128)(2,1)}, bf16[8,64,1024]{2,1,0:T(8,128)(2,1)S(1)}, u32[]{:S(2)}, u32[]{:S(2)}) collective-permute-start(bf16[8,64,1024]{2,1,0:T(8,128)(2,1)} %collective-permute-done.10.refs_1_), channel_id=1, source_target_pairs={{0,8},{8,0},{16,24},{24,16},{32,40},{40,32},{48,56},{56,48},{64,72... | collective-permute-start | bytes 3145736 | tf_op jit(solution)/shard_map/ppermute | solution.py:71
  274.3 14.1 %collective-permute-start.15 = (bf16[8,64,1024]{2,1,0:T(8,128)(2,1)}, bf16[8,64,1024]{2,1,0:T(8,128)(2,1)S(1)}, u32[]{:S(2)}, u32[]{:S(2)}) collective-permute-start(bf16[8,64,1024]{2,1,0:T(8,128)(2,1)} %collective-permute-done.13.refs_0_), channel_id=1, source_target_pairs={{0,8},{8,0},{16,24},{24,16},{32,40},{40,32},{48,56},{56,48},{64,72... | collective-permute-start | bytes 3145736 | tf_op jit(solution)/shard_map/ppermute | solution.py:71
  274.8 13.6 %collective-permute-start.16 = (bf16[8,64,1024]{2,1,0:T(8,128)(2,1)}, bf16[8,64,1024]{2,1,0:T(8,128)(2,1)S(1)}, u32[]{:S(2)}, u32[]{:S(2)}) collective-permute-start(bf16[8,64,1024]{2,1,0:T(8,128)(2,1)} %collective-permute-done.14.refs_1_), channel_id=1, source_target_pairs={{0,8},{8,0},{16,24},{24,16},{32,40},{40,32},{48,56},{56,48},{64,72... | collective-permute-start | bytes 3145736 | tf_op jit(solution)/shard_map/ppermute | solution.py:71
  (1 other events, 1.0 us)
Sparse Core Ops, SparseCore 0:
  10.0 247.9 all-gather.2

commit v2 on v0

v2 whole, which is shorter than its diff:
```python
import functools

import jax
import jax.numpy as jnp
from jax import lax
from jax.experimental import pallas as pl
from jax.experimental.pallas import tpu as pltpu
from jax.sharding import PartitionSpec as P

ROWS_LAST = (((1,), (1,)), ((), ()))


def after(value, *others):
    return lax.optimization_barrier((value, *others))[0]


def tiles_kernel(sizes, aliased, place_ref, *refs):
    pieces = sum(sizes)
    full_refs, piece_refs = refs[:2], refs[2 : 2 + 2 * pieces]
    out_ref = refs[2 + 2 * pieces + aliased]
    full, held, found, full_sem, held_sem, out_sem = refs[3 + 2 * pieces + aliased :]
    parts = full_refs[0].shape[0]
    count = held.shape[2]
    rows = count // 2

    full_copies = [
        pltpu.make_async_copy(full_refs[h].at[f], full.at[h * parts + f], full_sem.at[h * parts + f])
        for h in range(2)
        for f in range(parts)
    ]
    held_copies = [
        pltpu.make_async_copy(piece_refs[2 * i + h], held.at[i, pl.ds(h * parts, parts)], held_sem.at[2 * i + h])
        for i in range(pieces)
        for h in range(2)
    ]
    first = 2 * sizes[0]
    full_copies[0].start()
    for copy in held_copies[:first:2]:
        copy.start()
    for copy in full_copies[1:parts]:
        copy.start()
    for copy in held_copies[1:first:2]:
        copy.start()
    for copy in full_copies[parts:] + held_copies[first:]:
        copy.start()

    def out_copy(tile):
        return pltpu.make_async_copy(found.at[pl.ds(tile * rows, rows)], out_ref.at[place_ref[tile]], out_sem.at[tile])

    base = 0
    for g, size in enumerate(sizes):
        total = None
        for f in range(2 * parts):
            if g == 0:
                full_copies[f].wait()
            if f % parts == 0:
                for copy in held_copies[2 * base + f // parts : 2 * (base + size) : 2]:
                    copy.wait()
            lhs = jnp.concatenate([held[base + i, f] for i in range(size)], axis=0)
            part = lax.dot_general(lhs, full[f], ROWS_LAST, preferred_element_type=jnp.float32)
            total = part if total is None else total + part
        found[pl.ds(base * count, size * count)] = total
        for tile in range(2 * base, 2 * (base + size)):

            @pl.when(place_ref[tile] >= 0)
            def _(tile=tile):
                out_copy(tile).start()

        base += size
    for tile in range(2 * pieces):

        @pl.when(place_ref[tile] >= 0)
        def _(tile=tile):
            out_copy(tile).wait()


def tiles(place, near, far, groups, shape, out=None):
    parts, wide, depth = near.shape
    sizes = tuple(len(group) for group in groups)
    pieces = [half for group in groups for piece in group for half in piece]
    number = len(pieces) // 2
    count = pieces[0].shape[1]
    anywhere = pl.BlockSpec(memory_space=pl.ANY)
    given = [place, near, far, *pieces] + ([] if out is None else [out])
    return pl.pallas_call(
        functools.partial(tiles_kernel, sizes, 0 if out is None else 1),
        in_specs=[pl.BlockSpec(memory_space=pltpu.SMEM)] + [anywhere] * (len(given) - 1),
        out_specs=anywhere,
        out_shape=jax.ShapeDtypeStruct(shape, jnp.float32),
        input_output_aliases={} if out is None else {len(given) - 1: 0},
        scratch_shapes=[
            pltpu.VMEM((2 * parts, wide, depth), near.dtype),
            pltpu.VMEM((number, 2 * parts, count, depth), near.dtype),
            pltpu.VMEM((number * count, wide), jnp.float32),
            pltpu.SemaphoreType.DMA((2 * parts,)),
            pltpu.SemaphoreType.DMA((2 * number,)),
            pltpu.SemaphoreType.DMA((2 * number,)),
        ],
        compiler_params=pltpu.CompilerParams(vmem_limit_bytes=52 * 1024 * 1024),
        cost_estimate=pl.CostEstimate(
            flops=4 * parts * wide * depth * number * count,
            bytes_accessed=4 * parts * depth * (wide + number * count) + 4 * number * count * wide,
            transcendentals=0,
        ),
    )(*given)


def per_device(examples):
    blocks = lax.axis_size("ex")
    feats = lax.axis_size("feat")
    half = blocks // 2
    steps = blocks // 8
    ex = lax.axis_index("ex")
    core = ex % 2
    rows, depth = examples.shape
    line = feats // 2
    lines = [[q * line + x for x in range(line)] for q in range(2)]

    swap_pairs = [(i, i ^ 1) for i in range(blocks)]
    first_pairs = [(i, i - 2) for i in range(blocks) if i % 2 == 0 and i % half != 0]
    first_pairs += [(i, (i + half) % blocks) for i in range(blocks) if i % 2 == 1]
    wrap_pairs = [(1, half - 2), (half + 1, blocks - 2)]
    later_pairs = [(i, (i - 2 if i % 2 == 0 else i + 2) % blocks) for i in range(blocks)]
    wraps = (core == 0) & (ex % half == half - 2)

    def swap(piece):
        return lax.ppermute(piece, "ex", swap_pairs)

    near = lax.all_gather(examples, "feat", axis=0, axis_index_groups=lines)
    facing = lax.ppermute(examples, "feat", [(f, (f + line) % feats) for f in range(feats)])
    own = lax.all_to_all(examples.reshape(feats, rows // feats, depth), "feat", 0, 0)
    first = lax.axis_index("feat") < line
    own = after(own, facing)
    own_halves = [jnp.where(first, own[:line], own[line:]), jnp.where(first, own[line:], own[:line])]
    start = [jnp.concatenate([piece, swap(piece)], axis=1) for piece in own_halves]

    spots = [jnp.where(core == 0, 0, 1), jnp.where(core == 0, 1, 0)]
    for step in range(1, steps + 1):
        low, high = 2 * step, half + 2 - 2 * step
        mine, theirs = jnp.where(core == 0, low, high), jnp.where(core == 0, high, low)
        spots += [mine + core, mine + 1 - core, theirs + 1 - core, theirs + core]
    place = jnp.stack([jnp.where(spot - core > half, -1, spot - core) for spot in spots]).astype(jnp.int32)
    shape = (half + 1, rows // feats, rows)
    split = 2 + 4 * (steps - 1)

    turn = rows // feats
    held = start
    groups = [[start]]
    for step in range(steps):
        if step == 2:
            held = [after(held[0], near), held[1]]
        held = [lax.ppermute(piece, "ex", first_pairs if step == 0 else later_pairs) for piece in held]
        if step == 0:
            wrapped = [lax.ppermute(piece, "ex", wrap_pairs) for piece in held]
            held = [
                jnp.where(wraps, jnp.concatenate([new[:, turn:], new[:, :turn]], axis=1), piece)
                for new, piece in zip(wrapped, held)
            ]
            far = lax.all_gather(facing, "feat", axis=0, axis_index_groups=lines)
        if step == steps - 1:
            out = tiles(place[:split], near, far, groups, shape)
            held = [held[0], after(held[1], out)]
        groups.append([held, [swap(piece) for piece in held]])

    return tiles(place[split:], near, far, groups[-1:], shape, out)


def solution(mesh):
    placed = (P("ex", "feat"),)
    return jax.shard_map(
        per_device,
        mesh=mesh,
        in_specs=placed,
        out_specs=P(None, ("ex", "feat"), None),
        check_vma=False,
    )
```

time: 548 us -> 189 us (0.34)
  waiting for transfers between devices: 280 us -> 88.7 us
  starting transfers between devices: 188 us -> 56 us
  matrix products: 49.8 us -> 0 us
  Pallas kernels: 0 us -> 23.7 us
  other arithmetic: 12.1 us -> 3.37 us
    reduce_scatter x1 -> x0, waiting for transfers between devices: 217 us -> none  [per_device(): lax.psum_scatter(partial_value, 'feat', scatter_dimension=1, tiled=True)]
    ppermute x16 -> x21, starting transfers between devices: 188 us -> 51.9 us  [the longest x10 27.2 us: swap(): return lax.ppermute(piece, 'ex', swap_pairs)]
    dot_general x17 -> x0, matrix products: 49.8 us -> none  [product_with(): lax.dot_general(other, examples, (((1,), (1,)), ((), ())), preferred_elem...]
    all_to_all x0 -> x1, waiting for transfers between devices: none -> 29.3 us  [per_device(): lax.all_to_all(examples.reshape(feats, rows // feats, depth), 'feat', 0, 0)]
    pallas_call x0 -> x2, Pallas kernels: none -> 23.7 us  [tiles(): pl.pallas_call(functools.partial(tiles_kernel, sizes, 0 if out is None el...]
    concatenate x1 -> x2, other arithmetic: 12.1 us -> 1.14 us  [per_device(): jnp.concatenate([piece, swap(piece)], axis=1)]
    ppermute x16 -> x21, waiting for transfers between devices: 63.2 us -> 58.7 us  [the longest x8 40.4 us: per_device(): lax.ppermute(piece, 'ex', first_pairs if step == 0 else later_pairs)]
  transfers between devices with their start and end apart: 17 -> 24, of which waited for: 17 -> 11; matrix products, arithmetic and copies ran while one was open for 0% -> 3% of each run, Pallas kernels for 0% -> 9%
where the time goes in v2:
time: 189 us
  waiting for transfers between devices  88.7 us (47%)
  starting transfers between devices  56 us (30%)
  Pallas kernels  23.7 us (13%)
  between operations  13.6 us (7%)
  local copies, waits for them, and re-layouts  3.37 us (2%)
  other arithmetic  3.37 us (2%)
    ppermute x8, waiting for transfers between devices, per_device(): lax.ppermute(piece, 'ex', first_pairs if step == 0 else later_pairs)  40.4 us
    all_to_all x1, waiting for transfers between devices, per_device(): lax.all_to_all(examples.reshape(feats, rows // feats, depth), 'feat', 0, 0)  29.3 us
    ppermute x10, starting transfers between devices, swap(): return lax.ppermute(piece, 'ex', swap_pairs)  27.2 us
    pallas_call x2, Pallas kernels, tiles(): pl.pallas_call(functools.partial(tiles_kernel, sizes, 0 if out is None el...  23.7 us
    ppermute x2, starting transfers between devices, per_device(): wrapped = [lax.ppermute(piece, 'ex', wrap_pairs) for piece in held]  15.4 us
    ppermute x2, waiting for transfers between devices, per_device(): wrapped = [lax.ppermute(piece, 'ex', wrap_pairs) for piece in held]  14 us
    ppermute x8, starting transfers between devices, per_device(): lax.ppermute(piece, 'ex', first_pairs if step == 0 else later_pairs)  5.53 us
    ppermute x10, waiting for transfers between devices, swap(): return lax.ppermute(piece, 'ex', swap_pairs)  4.31 us
  transfers between devices with their start and end apart: 24, of which 11 were waited for; matrix products, arithmetic and copies ran while one was open for 3% of the time, Pallas kernels for 9%

profile of v2, /device:TPU:1, one launch (start us, length us, event | category | flops | bytes accessed | tf_op | source)
XLA Modules:
  0.0 188.8 jit_solution(7229914149925421124)
XLA Ops:
  7.3 3.8 %collective-permute-start = (bf16[512,1024]{1,0:T(8,128)(2,1)}, bf16[512,1024]{1,0:T(8,128)(2,1)S(1)}, u32[]{:S(2)}, u32[]{:S(2)}) collective-permute-start(bf16[512,1024]{1,0:T(8,128)(2,1)} %param.1), channel_id=1, source_target_pairs={{0,4},{1,5},{2,6},{3,7},{4,0},{5,1},{6,2},{7,3},{8,12},{9,13},{10,... | collective-permute-start | bytes 3145736 | tf_op jit(solution)/shard_map/ppermute | solution.py:130
  11.1 4.0 %all-to-all-start = ((bf16[8,64,1024]{2,1,0:T(8,128)(2,1)}), bf16[8,64,1024]{2,1,0:T(8,128)(2,1)S(1)}, u32[]{:S(2)}, u32[]{:S(2)}) async-start(bf16[8,64,1024]{2,1,0:T(8,128)(2,1)} %bitcast.25), calls=%async_computation | async-start | bytes 2097152 | tf_op jit(solution)/shard_map/all_to_all | solution.py:131
  15.2 29.3 %all-to-all-done = bf16[8,64,1024]{2,1,0:T(8,128)(2,1)S(1)} async-done(((bf16[8,64,1024]{2,1,0:T(8,128)(2,1)}), bf16[8,64,1024]{2,1,0:T(8,128)(2,1)S(1)}, u32[]{:S(2)}, u32[]{:S(2)}) %all-to-all-start) | async-done | bytes 1048608 | tf_op jit(solution)/shard_map/all_to_all | solution.py:131
  44.5 2.3 %collective-permute-start.7 = (bf16[4,64,1024]{2,1,0:T(8,128)(2,1)S(1)}, bf16[4,64,1024]{2,1,0:T(8,128)(2,1)S(1)}, u32[]{:S(2)}, u32[]{:S(2)}) collective-permute-start(bf16[4,64,1024]{2,1,0:T(8,128)(2,1)S(1)} %get-tuple-element.13), channel_id=1, source_target_pairs={{0,8},{8,0},{16,24},{24,16},{32,40},{40,32},{48,56},{56,48},{64,72... | collective-permute-start | bytes 1572872 | tf_op jit(solution)/shard_map/ppermute | solution.py:127
  49.4 3.2 %collective-permute-start.8 = (bf16[4,128,1024]{2,1,0:T(8,128)(2,1)}, bf16[4,128,1024]{2,1,0:T(8,128)(2,1)}, u32[]{:S(2)}, u32[]{:S(2)}) collective-permute-start(bf16[4,128,1024]{2,1,0:T(8,128)(2,1)} %pad_maximum_fusion.1.refs_3_), channel_id=1, source_target_pairs={{16,0},{32,16},{48,32},{64,48},{80,64},{96,80},{112,96},{144,128},... | collective-permute-start | bytes 3145736 | tf_op jit(solution)/shard_map/ppermute | solution.py:152
  52.8 2.0 %collective-permute-start.2 = (bf16[4,128,1024]{2,1,0:T(8,128)(2,1)S(1)}, bf16[4,128,1024]{2,1,0:T(8,128)(2,1)S(1)}, u32[]{:S(2)}, u32[]{:S(2)}) collective-permute-start(bf16[4,128,1024]{2,1,0:T(8,128)(2,1)S(1)} %pad_maximum_fusion.refs_2_), channel_id=1, source_target_pairs={{16,0},{32,16},{48,32},{64,48},{80,64},{96,80},{112,96},{144,128},... | collective-permute-start | bytes 3145736 | tf_op jit(solution)/shard_map/ppermute | solution.py:152
  54.8 10.7 %collective-permute-done.8 = bf16[4,128,1024]{2,1,0:T(8,128)(2,1)} collective-permute-done((bf16[4,128,1024]{2,1,0:T(8,128)(2,1)}, bf16[4,128,1024]{2,1,0:T(8,128)(2,1)}, u32[]{:S(2)}, u32[]{:S(2)}) %collective-permute-start.8) | collective-permute-done | bytes 1048608 | tf_op jit(solution)/shard_map/ppermute | solution.py:152
  65.6 7.2 %collective-permute-start.9 = (bf16[4,128,1024]{2,1,0:T(8,128)(2,1)}, bf16[4,128,1024]{2,1,0:T(8,128)(2,1)S(1)}, u32[]{:S(2)}, u32[]{:S(2)}) collective-permute-start(bf16[4,128,1024]{2,1,0:T(8,128)(2,1)} %collective-permute-done.8), channel_id=1, source_target_pairs={{8,112},{136,240},{9,113},{137,241},{10,114},{138,242},{11,115},{1... | collective-permute-start | bytes 3145736 | tf_op jit(solution)/shard_map/ppermute | solution.py:154
  72.8 3.9 %collective-permute-done.2 = bf16[4,128,1024]{2,1,0:T(8,128)(2,1)S(1)} collective-permute-done((bf16[4,128,1024]{2,1,0:T(8,128)(2,1)S(1)}, bf16[4,128,1024]{2,1,0:T(8,128)(2,1)S(1)}, u32[]{:S(2)}, u32[]{:S(2)}) %collective-permute-start.2) | collective-permute-done | bytes 1048608 | tf_op jit(solution)/shard_map/ppermute | solution.py:152
  76.7 8.1 %collective-permute-start.3 = (bf16[4,128,1024]{2,1,0:T(8,128)(2,1)S(1)}, bf16[4,128,1024]{2,1,0:T(8,128)(2,1)}, u32[]{:S(2)}, u32[]{:S(2)}) collective-permute-start(bf16[4,128,1024]{2,1,0:T(8,128)(2,1)S(1)} %collective-permute-done.2), channel_id=1, source_target_pairs={{8,112},{136,240},{9,113},{137,241},{10,114},{138,242},{11,115},{1... | collective-permute-start | bytes 3145736 | tf_op jit(solution)/shard_map/ppermute | solution.py:154
  84.9 1.7 maximum_select_fusion.1.refs_5_
  86.7 14.0 %collective-permute-done.3 = bf16[4,128,1024]{2,1,0:T(8,128)(2,1)} collective-permute-done((bf16[4,128,1024]{2,1,0:T(8,128)(2,1)S(1)}, bf16[4,128,1024]{2,1,0:T(8,128)(2,1)}, u32[]{:S(2)}, u32[]{:S(2)}) %collective-permute-start.3) | collective-permute-done | bytes 1048608 | tf_op jit(solution)/shard_map/ppermute | solution.py:154
  102.5 6.3 %collective-permute-start.14 = (bf16[4,128,1024]{2,1,0:T(8,128)(2,1)S(1)}, bf16[4,128,1024]{2,1,0:T(8,128)(2,1)}, u32[]{:S(2)}, u32[]{:S(2)}) collective-permute-start(bf16[4,128,1024]{2,1,0:T(8,128)(2,1)S(1)} %maximum_select_fusion.1.refs_5_), channel_id=1, source_target_pairs={{0,8},{8,0},{16,24},{24,16},{32,40},{40,32},{48,56},{56,48},{64,72... | collective-permute-start | bytes 3145736 | tf_op jit(solution)/shard_map/ppermute | solution.py:127
  108.9 9.5 %collective-permute-done.4.refs_8_ = bf16[4,128,1024]{2,1,0:T(8,128)(2,1)} collective-permute-done((bf16[4,128,1024]{2,1,0:T(8,128)(2,1)S(1)}, bf16[4,128,1024]{2,1,0:T(8,128)(2,1)}, u32[]{:S(2)}, u32[]{:S(2)}) %collective-permute-start.4) | collective-permute-done | bytes 1048608 | tf_op jit(solution)/shard_map/ppermute | solution.py:152
  118.4 7.5 %collective-permute-start.13 = (bf16[4,128,1024]{2,1,0:T(8,128)(2,1)S(1)}, bf16[4,128,1024]{2,1,0:T(8,128)(2,1)S(1)}, u32[]{:S(2)}, u32[]{:S(2)}) collective-permute-start(bf16[4,128,1024]{2,1,0:T(8,128)(2,1)S(1)} %maximum_select_fusion.refs_4_), channel_id=1, source_target_pairs={{0,8},{8,0},{16,24},{24,16},{32,40},{40,32},{48,56},{56,48},{64,72... | collective-permute-start | bytes 3145736 | tf_op jit(solution)/shard_map/ppermute | solution.py:127
  126.4 3.2 %collective-permute-done.11.refs_13_ = bf16[4,128,1024]{2,1,0:T(8,128)(2,1)} collective-permute-done((bf16[4,128,1024]{2,1,0:T(8,128)(2,1)}, bf16[4,128,1024]{2,1,0:T(8,128)(2,1)}, u32[]{:S(2)}, u32[]{:S(2)}) %collective-permute-start.11) | collective-permute-done | bytes 1048608 | tf_op jit(solution)/shard_map/ppermute | solution.py:152
  129.6 2.9 %collective-permute-start.18 = (bf16[4,128,1024]{2,1,0:T(8,128)(2,1)}, bf16[4,128,1024]{2,1,0:T(8,128)(2,1)}, u32[]{:S(2)}, u32[]{:S(2)}) collective-permute-start(bf16[4,128,1024]{2,1,0:T(8,128)(2,1)} %collective-permute-done.11.refs_13_), channel_id=1, source_target_pairs={{0,8},{8,0},{16,24},{24,16},{32,40},{40,32},{48,56},{56,48},{64,72... | collective-permute-start | bytes 3145736 | tf_op jit(solution)/shard_map/ppermute | solution.py:127
  132.5 8.3 %collective-permute-done.5.refs_12_ = bf16[4,128,1024]{2,1,0:T(8,128)(2,1)} collective-permute-done((bf16[4,128,1024]{2,1,0:T(8,128)(2,1)}, bf16[4,128,1024]{2,1,0:T(8,128)(2,1)}, u32[]{:S(2)}, u32[]{:S(2)}) %collective-permute-start.5) | collective-permute-done | bytes 1048608 | tf_op jit(solution)/shard_map/ppermute | solution.py:152
  140.8 2.9 %collective-permute-start.17 = (bf16[4,128,1024]{2,1,0:T(8,128)(2,1)}, bf16[4,128,1024]{2,1,0:T(8,128)(2,1)}, u32[]{:S(2)}, u32[]{:S(2)}) collective-permute-start(bf16[4,128,1024]{2,1,0:T(8,128)(2,1)} %collective-permute-done.5.refs_12_), channel_id=1, source_target_pairs={{0,8},{8,0},{16,24},{24,16},{32,40},{40,32},{48,56},{56,48},{64,72... | collective-permute-start | bytes 3145736 | tf_op jit(solution)/shard_map/ppermute | solution.py:127
  146.4 16.5 %shard_map.17.refs_6_ = f32[17,64,512]{2,1,0:T(8,128)} custom-call(s32[14]{0:T(128)S(1)} %stack.79.place_ref, bf16[4,512,1024]{2,1,0:T(8,128)(2,1)} %bitcast.21, bf16[4,512,1024]{2,1,0:T(8,128)(2,1)} %bitcast.23, bf16[4,128,1024]{2,1,0:T(8,128)(2,1)S(1)} %pad_maximum_fusion.refs_2_, bf16[4,128,1024]{2,1,0:T(8,128)(2,1)} %pad_maximum_fusion.1.refs_3_, ...), custom_call_target="tpu_custom_call" | custom-call | flops 7516192768 | bytes 24903680 | tf_op jit(solution)/shard_map/pallas_call | solution.py:85
  162.9 4.2 %collective-permute-start.20 = (bf16[4,128,1024]{2,1,0:T(8,128)(2,1)S(1)}, bf16[4,128,1024]{2,1,0:T(8,128)(2,1)}, u32[]{:S(2)}, u32[]{:S(2)}) collective-permute-start(bf16[4,128,1024]{2,1,0:T(8,128)(2,1)S(1)} %collective-permute-done.12.refs_3_), channel_id=1, source_target_pairs={{0,8},{8,0},{16,24},{24,16},{32,40},{40,32},{48,56},{56,48},{64,72... | collective-permute-start | bytes 3145736 | tf_op jit(solution)/shard_map/ppermute | solution.py:127
  167.1 4.7 %collective-permute-done.6.refs_2_ = bf16[4,128,1024]{2,1,0:T(8,128)(2,1)S(1)} collective-permute-done((bf16[4,128,1024]{2,1,0:T(8,128)(2,1)}, bf16[4,128,1024]{2,1,0:T(8,128)(2,1)S(1)}, u32[]{:S(2)}, u32[]{:S(2)}) %collective-permute-start.6) | collective-permute-done | bytes 1048608 | tf_op jit(solution)/shard_map/ppermute | solution.py:152
  172.4 2.3 %collective-permute-done.19.refs_4_ = bf16[4,128,1024]{2,1,0:T(8,128)(2,1)} collective-permute-done((bf16[4,128,1024]{2,1,0:T(8,128)(2,1)S(1)}, bf16[4,128,1024]{2,1,0:T(8,128)(2,1)}, u32[]{:S(2)}, u32[]{:S(2)}) %collective-permute-start.19) | collective-permute-done | bytes 1048608 | tf_op jit(solution)/shard_map/ppermute | solution.py:127
  174.7 7.3 %shard_map.18 = f32[17,64,512]{2,1,0:T(8,128)} custom-call(s32[4]{0:T(128)S(1)} %pad_add_fusion.place_ref, bf16[4,512,1024]{2,1,0:T(8,128)(2,1)} %bitcast.22, bf16[4,512,1024]{2,1,0:T(8,128)(2,1)} %bitcast.24, bf16[4,128,1024]{2,1,0:T(8,128)(2,1)S(1)} %collective-permute-done.6.refs_2_, ...), custom_call_target="tpu_custom_call", output_to_operand_aliasing={{}: (7, {})} | custom-call | flops 2147483648 | bytes 13107200 | tf_op jit(solution)/shard_map/pallas_call | solution.py:85
  (53 shorter events, 9.3 us)
Async XLA Ops:
  6.5 111.8 %all-gather.5.cloned.1.call-start = ((), (), s32[]{:S(2)}) async-start(), calls=%async_computation.1 | async-start | bytes 5242880 | tf_op jit(solution)/shard_map/all_gather | solution.py:129
  7.3 37.2 %collective-permute-start = (bf16[512,1024]{1,0:T(8,128)(2,1)}, bf16[512,1024]{1,0:T(8,128)(2,1)S(1)}, u32[]{:S(2)}, u32[]{:S(2)}) collective-permute-start(bf16[512,1024]{1,0:T(8,128)(2,1)} %param.1), channel_id=1, source_target_pairs={{0,4},{1,5},{2,6},{3,7},{4,0},{5,1},{6,2},{7,3},{8,12},{9,13},{10,... | collective-permute-start | bytes 3145736 | tf_op jit(solution)/shard_map/ppermute | solution.py:130
  11.1 33.4 %all-to-all-start = ((bf16[8,64,1024]{2,1,0:T(8,128)(2,1)}), bf16[8,64,1024]{2,1,0:T(8,128)(2,1)S(1)}, u32[]{:S(2)}, u32[]{:S(2)}) async-start(bf16[8,64,1024]{2,1,0:T(8,128)(2,1)} %bitcast.25), calls=%async_computation | async-start | bytes 2097152 | tf_op jit(solution)/shard_map/all_to_all | solution.py:131
  15.1 130.7 %all-gather.7.cloned.1.call-start = ((), (), s32[]{:S(2)}) async-start(), calls=%async_computation.2 | async-start | bytes 5242880 | tf_op jit(solution)/shard_map/all_gather | solution.py:159
  44.5 3.8 %collective-permute-start.7 = (bf16[4,64,1024]{2,1,0:T(8,128)(2,1)S(1)}, bf16[4,64,1024]{2,1,0:T(8,128)(2,1)S(1)}, u32[]{:S(2)}, u32[]{:S(2)}) collective-permute-start(bf16[4,64,1024]{2,1,0:T(8,128)(2,1)S(1)} %get-tuple-element.13), channel_id=1, source_target_pairs={{0,8},{8,0},{16,24},{24,16},{32,40},{40,32},{48,56},{56,48},{64,72... | collective-permute-start | bytes 1572872 | tf_op jit(solution)/shard_map/ppermute | solution.py:127
  46.8 5.9 %collective-permute-start.1 = (bf16[4,64,1024]{2,1,0:T(8,128)(2,1)S(1)}, bf16[4,64,1024]{2,1,0:T(8,128)(2,1)S(1)}, u32[]{:S(2)}, u32[]{:S(2)}) collective-permute-start(bf16[4,64,1024]{2,1,0:T(8,128)(2,1)S(1)} %get-tuple-element.14), channel_id=1, source_target_pairs={{0,8},{8,0},{16,24},{24,16},{32,40},{40,32},{48,56},{56,48},{64,72... | collective-permute-start | bytes 1572872 | tf_op jit(solution)/shard_map/ppermute | solution.py:127
  49.4 16.1 %collective-permute-start.8 = (bf16[4,128,1024]{2,1,0:T(8,128)(2,1)}, bf16[4,128,1024]{2,1,0:T(8,128)(2,1)}, u32[]{:S(2)}, u32[]{:S(2)}) collective-permute-start(bf16[4,128,1024]{2,1,0:T(8,128)(2,1)} %pad_maximum_fusion.1.refs_3_), channel_id=1, source_target_pairs={{16,0},{32,16},{48,32},{64,48},{80,64},{96,80},{112,96},{144,128},... | collective-permute-start | bytes 3145736 | tf_op jit(solution)/shard_map/ppermute | solution.py:152
  52.8 23.9 %collective-permute-start.2 = (bf16[4,128,1024]{2,1,0:T(8,128)(2,1)S(1)}, bf16[4,128,1024]{2,1,0:T(8,128)(2,1)S(1)}, u32[]{:S(2)}, u32[]{:S(2)}) collective-permute-start(bf16[4,128,1024]{2,1,0:T(8,128)(2,1)S(1)} %pad_maximum_fusion.refs_2_), channel_id=1, source_target_pairs={{16,0},{32,16},{48,32},{64,48},{80,64},{96,80},{112,96},{144,128},... | collective-permute-start | bytes 3145736 | tf_op jit(solution)/shard_map/ppermute | solution.py:152
  65.6 19.3 %collective-permute-start.9 = (bf16[4,128,1024]{2,1,0:T(8,128)(2,1)}, bf16[4,128,1024]{2,1,0:T(8,128)(2,1)S(1)}, u32[]{:S(2)}, u32[]{:S(2)}) collective-permute-start(bf16[4,128,1024]{2,1,0:T(8,128)(2,1)} %collective-permute-done.8), channel_id=1, source_target_pairs={{8,112},{136,240},{9,113},{137,241},{10,114},{138,242},{11,115},{1... | collective-permute-start | bytes 3145736 | tf_op jit(solution)/shard_map/ppermute | solution.py:154
  76.7 24.0 %collective-permute-start.3 = (bf16[4,128,1024]{2,1,0:T(8,128)(2,1)S(1)}, bf16[4,128,1024]{2,1,0:T(8,128)(2,1)}, u32[]{:S(2)}, u32[]{:S(2)}) collective-permute-start(bf16[4,128,1024]{2,1,0:T(8,128)(2,1)S(1)} %collective-permute-done.2), channel_id=1, source_target_pairs={{8,112},{136,240},{9,113},{137,241},{10,114},{138,242},{11,115},{1... | collective-permute-start | bytes 3145736 | tf_op jit(solution)/shard_map/ppermute | solution.py:154
  86.6 22.3 %collective-permute-start.10 = (bf16[4,128,1024]{2,1,0:T(8,128)(2,1)S(1)}, bf16[4,128,1024]{2,1,0:T(8,128)(2,1)}, u32[]{:S(2)}, u32[]{:S(2)}) collective-permute-start(bf16[4,128,1024]{2,1,0:T(8,128)(2,1)S(1)} %maximum_select_fusion.1.refs_5_), channel_id=1, source_target_pairs={{0,240},{8,24},{16,0},{24,40},{32,16},{40,56},{48,32},{56,72},{64,... | collective-permute-start | bytes 3145736 | tf_op jit(solution)/shard_map/ppermute | solution.py:152
  102.4 15.9 %collective-permute-start.4 = (bf16[4,128,1024]{2,1,0:T(8,128)(2,1)S(1)}, bf16[4,128,1024]{2,1,0:T(8,128)(2,1)}, u32[]{:S(2)}, u32[]{:S(2)}) collective-permute-start(bf16[4,128,1024]{2,1,0:T(8,128)(2,1)S(1)} %maximum_select_fusion.refs_4_), channel_id=1, source_target_pairs={{0,240},{8,24},{16,0},{24,40},{32,16},{40,56},{48,32},{56,72},{64,... | collective-permute-start | bytes 3145736 | tf_op jit(solution)/shard_map/ppermute | solution.py:152
  102.5 23.3 %collective-permute-start.14 = (bf16[4,128,1024]{2,1,0:T(8,128)(2,1)S(1)}, bf16[4,128,1024]{2,1,0:T(8,128)(2,1)}, u32[]{:S(2)}, u32[]{:S(2)}) collective-permute-start(bf16[4,128,1024]{2,1,0:T(8,128)(2,1)S(1)} %maximum_select_fusion.1.refs_5_), channel_id=1, source_target_pairs={{0,8},{8,0},{16,24},{24,16},{32,40},{40,32},{48,56},{56,48},{64,72... | collective-permute-start | bytes 3145736 | tf_op jit(solution)/shard_map/ppermute | solution.py:127
  108.9 20.7 %collective-permute-start.11 = (bf16[4,128,1024]{2,1,0:T(8,128)(2,1)}, bf16[4,128,1024]{2,1,0:T(8,128)(2,1)}, u32[]{:S(2)}, u32[]{:S(2)}) collective-permute-start(bf16[4,128,1024]{2,1,0:T(8,128)(2,1)} %collective-permute-done.10.refs_9_), channel_id=1, source_target_pairs={{0,240},{8,24},{16,0},{24,40},{32,16},{40,56},{48,32},{56,72},{64,... | collective-permute-start | bytes 3145736 | tf_op jit(solution)/shard_map/ppermute | solution.py:152
  118.4 22.5 %collective-permute-start.5 = (bf16[4,128,1024]{2,1,0:T(8,128)(2,1)}, bf16[4,128,1024]{2,1,0:T(8,128)(2,1)}, u32[]{:S(2)}, u32[]{:S(2)}) collective-permute-start(bf16[4,128,1024]{2,1,0:T(8,128)(2,1)} %collective-permute-done.4.refs_8_), channel_id=1, source_target_pairs={{0,240},{8,24},{16,0},{24,40},{32,16},{40,56},{48,32},{56,72},{64,... | collective-permute-start | bytes 3145736 | tf_op jit(solution)/shard_map/ppermute | solution.py:152
  118.4 25.4 %collective-permute-start.13 = (bf16[4,128,1024]{2,1,0:T(8,128)(2,1)S(1)}, bf16[4,128,1024]{2,1,0:T(8,128)(2,1)S(1)}, u32[]{:S(2)}, u32[]{:S(2)}) collective-permute-start(bf16[4,128,1024]{2,1,0:T(8,128)(2,1)S(1)} %maximum_select_fusion.refs_4_), channel_id=1, source_target_pairs={{0,8},{8,0},{16,24},{24,16},{32,40},{40,32},{48,56},{56,48},{64,72... | collective-permute-start | bytes 3145736 | tf_op jit(solution)/shard_map/ppermute | solution.py:127
  125.9 18.9 %collective-permute-start.16 = (bf16[4,128,1024]{2,1,0:T(8,128)(2,1)}, bf16[4,128,1024]{2,1,0:T(8,128)(2,1)S(1)}, u32[]{:S(2)}, u32[]{:S(2)}) collective-permute-start(bf16[4,128,1024]{2,1,0:T(8,128)(2,1)} %collective-permute-done.10.refs_9_), channel_id=1, source_target_pairs={{0,8},{8,0},{16,24},{24,16},{32,40},{40,32},{48,56},{56,48},{64,72... | collective-permute-start | bytes 3145736 | tf_op jit(solution)/shard_map/ppermute | solution.py:127
  125.9 19.9 %collective-permute-start.15 = (bf16[4,128,1024]{2,1,0:T(8,128)(2,1)}, bf16[4,128,1024]{2,1,0:T(8,128)(2,1)}, u32[]{:S(2)}, u32[]{:S(2)}) collective-permute-start(bf16[4,128,1024]{2,1,0:T(8,128)(2,1)} %collective-permute-done.4.refs_8_), channel_id=1, source_target_pairs={{0,8},{8,0},{16,24},{24,16},{32,40},{40,32},{48,56},{56,48},{64,72... | collective-permute-start | bytes 3145736 | tf_op jit(solution)/shard_map/ppermute | solution.py:127
  129.6 16.2 %collective-permute-start.18 = (bf16[4,128,1024]{2,1,0:T(8,128)(2,1)}, bf16[4,128,1024]{2,1,0:T(8,128)(2,1)}, u32[]{:S(2)}, u32[]{:S(2)}) collective-permute-start(bf16[4,128,1024]{2,1,0:T(8,128)(2,1)} %collective-permute-done.11.refs_13_), channel_id=1, source_target_pairs={{0,8},{8,0},{16,24},{24,16},{32,40},{40,32},{48,56},{56,48},{64,72... | collective-permute-start | bytes 3145736 | tf_op jit(solution)/shard_map/ppermute | solution.py:127
  140.8 5.5 %collective-permute-start.17 = (bf16[4,128,1024]{2,1,0:T(8,128)(2,1)}, bf16[4,128,1024]{2,1,0:T(8,128)(2,1)}, u32[]{:S(2)}, u32[]{:S(2)}) collective-permute-start(bf16[4,128,1024]{2,1,0:T(8,128)(2,1)} %collective-permute-done.5.refs_12_), channel_id=1, source_target_pairs={{0,8},{8,0},{16,24},{24,16},{32,40},{40,32},{48,56},{56,48},{64,72... | collective-permute-start | bytes 3145736 | tf_op jit(solution)/shard_map/ppermute | solution.py:127
  143.8 19.1 %collective-permute-start.12 = (bf16[4,128,1024]{2,1,0:T(8,128)(2,1)}, bf16[4,128,1024]{2,1,0:T(8,128)(2,1)S(1)}, u32[]{:S(2)}, u32[]{:S(2)}) collective-permute-start(bf16[4,128,1024]{2,1,0:T(8,128)(2,1)} %collective-permute-done.11.refs_13_), channel_id=1, source_target_pairs={{0,240},{8,24},{16,0},{24,40},{32,16},{40,56},{48,32},{56,72},{64,... | collective-permute-start | bytes 3145736 | tf_op jit(solution)/shard_map/ppermute | solution.py:152
  145.7 26.1 %collective-permute-start.6 = (bf16[4,128,1024]{2,1,0:T(8,128)(2,1)}, bf16[4,128,1024]{2,1,0:T(8,128)(2,1)S(1)}, u32[]{:S(2)}, u32[]{:S(2)}) collective-permute-start(bf16[4,128,1024]{2,1,0:T(8,128)(2,1)} %collective-permute-done.5.refs_12_), channel_id=1, source_target_pairs={{0,240},{8,24},{16,0},{24,40},{32,16},{40,56},{48,32},{56,72},{64,... | collective-permute-start | bytes 3145736 | tf_op jit(solution)/shard_map/ppermute | solution.py:152
  162.9 9.5 %collective-permute-start.20 = (bf16[4,128,1024]{2,1,0:T(8,128)(2,1)S(1)}, bf16[4,128,1024]{2,1,0:T(8,128)(2,1)}, u32[]{:S(2)}, u32[]{:S(2)}) collective-permute-start(bf16[4,128,1024]{2,1,0:T(8,128)(2,1)S(1)} %collective-permute-done.12.refs_3_), channel_id=1, source_target_pairs={{0,8},{8,0},{16,24},{24,16},{32,40},{40,32},{48,56},{56,48},{64,72... | collective-permute-start | bytes 3145736 | tf_op jit(solution)/shard_map/ppermute | solution.py:127
  171.8 3.0 %collective-permute-start.19 = (bf16[4,128,1024]{2,1,0:T(8,128)(2,1)S(1)}, bf16[4,128,1024]{2,1,0:T(8,128)(2,1)}, u32[]{:S(2)}, u32[]{:S(2)}) collective-permute-start(bf16[4,128,1024]{2,1,0:T(8,128)(2,1)S(1)} %collective-permute-done.6.refs_2_), channel_id=1, source_target_pairs={{0,8},{8,0},{16,24},{24,16},{32,40},{40,32},{48,56},{56,48},{64,72... | collective-permute-start | bytes 3145736 | tf_op jit(solution)/shard_map/ppermute | solution.py:127
  (8 other events, 101.2 us)
Sparse Core Ops, SparseCore 0:
  9.2 55.2 all-gather.4
  66.3 52.2 all-gather.6

commit v3 on v2

--- a/solution.py
+++ b/solution.py
@@ -105,6 +105,88 @@
     )(*given)
 
 
+def half_kernel(final, *refs):
+    place_ref, refs = (refs[0], refs[1:]) if final else (None, refs)
+    full_ref, here_ref, there_ref = refs[:3]
+    sums_ref = refs[3] if final else None
+    out_ref = refs[5] if final else refs[3]
+    full, held, found, sums, full_sem, held_sem, sums_sem, out_sem = refs[6 if final else 4 :]
+    parts, count = full.shape[0], held.shape[1] // 2
+    rows = count // 2
+
+    full_copies = [pltpu.make_async_copy(full_ref.at[f], full.at[f], full_sem.at[f]) for f in range(parts)]
+    held_copies = [
+        pltpu.make_async_copy(ref.at[f], held.at[f, pl.ds(i * count, count)], held_sem.at[i * parts + f])
+        for i, ref in enumerate((here_ref, there_ref))
+        for f in range(parts)
+    ]
+    for f in range(parts):
+        for copy in (full_copies[f], held_copies[f], held_copies[parts + f]):
+            copy.start()
+    if final:
+        sums_copy = pltpu.make_async_copy(sums_ref, sums, sums_sem)
+        sums_copy.start()
+    total = None
+    for f in range(parts):
+        for copy in (full_copies[f], held_copies[f], held_copies[parts + f]):
+            copy.wait()
+        part = lax.dot_general(held[f], full[f], ROWS_LAST, preferred_element_type=jnp.float32)
+        total = part if total is None else total + part
+    if final:
+        sums_copy.wait()
+        found[...] = total + sums[...]
+        for tile in range(4):
+            copy = pltpu.make_async_copy(
+                found.at[pl.ds(tile * rows, rows)], out_ref.at[place_ref[tile]], out_sem.at[tile]
+            )
+            copy.start()
+        for tile in range(4):
+            copy = pltpu.make_async_copy(
+                found.at[pl.ds(tile * rows, rows)], out_ref.at[place_ref[tile]], out_sem.at[tile]
+            )
+            copy.wait()
+    else:
+        found[...] = total
+        copy = pltpu.make_async_copy(found, out_ref, sums_sem)
+        copy.start()
+        copy.wait()
+
+
+def half_tiles(full, pieces, place=None, sums=None, out=None):
+    parts, wide, depth = full.shape
+    count = 2 * pieces[0].shape[1]
+    final = out is not None
+    anywhere = pl.BlockSpec(memory_space=pl.ANY)
+    given = [place, full, *pieces, sums, out] if final else [full, *pieces]
+    specs = [anywhere] * len(given)
+    if final:
+        specs[0] = pl.BlockSpec(memory_space=pltpu.SMEM)
+    shape = out.shape if final else (count, wide)
+    return pl.pallas_call(
+        functools.partial(half_kernel, final),
+        in_specs=specs,
+        out_specs=anywhere,
+        out_shape=jax.ShapeDtypeStruct(shape, jnp.float32),
+        input_output_aliases={5: 0} if final else {},
+        scratch_shapes=[
+            pltpu.VMEM((parts, wide, depth), full.dtype),
+            pltpu.VMEM((parts, count, depth), full.dtype),
+            pltpu.VMEM((count, wide), jnp.float32),
+            pltpu.VMEM((count, wide), jnp.float32),
+            pltpu.SemaphoreType.DMA((parts,)),
+            pltpu.SemaphoreType.DMA((2 * parts,)),
+            pltpu.SemaphoreType.DMA,
+            pltpu.SemaphoreType.DMA((4,)),
+        ],
+        compiler_params=pltpu.CompilerParams(vmem_limit_bytes=52 * 1024 * 1024),
+        cost_estimate=pl.CostEstimate(
+            flops=2 * parts * wide * depth * count,
+            bytes_accessed=2 * parts * depth * (wide + count) + 4 * count * wide,
+            transcendentals=0,
+        ),
+    )(*given)
+
+
 def per_device(examples):
     blocks = lax.axis_size("ex")
     feats = lax.axis_size("feat")
@@ -149,6 +231,10 @@
     for step in range(steps):
         if step == 2:
             held = [after(held[0], near), held[1]]
+        if step == steps - 1:
+            early = 2 + 4 * (steps - 2)
+            out = tiles(place[:early], near, far, groups[:-1], shape)
+            held = [held[0], after(held[1], out)]
         held = [lax.ppermute(piece, "ex", first_pairs if step == 0 else later_pairs) for piece in held]
         if step == 0:
             wrapped = [lax.ppermute(piece, "ex", wrap_pairs) for piece in held]
@@ -158,11 +244,12 @@
             ]
             far = lax.all_gather(facing, "feat", axis=0, axis_index_groups=lines)
         if step == steps - 1:
-            out = tiles(place[:split], near, far, groups, shape)
-            held = [held[0], after(held[1], out)]
+            across = swap(held[1])
+            out = tiles(place[early:split], near, far, groups[-1:], shape, out)
+            sums = half_tiles(far, [held[1], across])
+            last = after(held[0], out)
+            return half_tiles(near, [last, swap(last)], place[split:], sums, out)
         groups.append([held, [swap(piece) for piece in held]])
-
-    return tiles(place[split:], near, far, groups[-1:], shape, out)
 
 
 def solution(mesh):

time: 189 us -> 186 us (0.984)
  starting transfers between devices: 56 us -> 44.5 us
  waiting for transfers between devices: 88.7 us -> 93.4 us
  Pallas kernels: 23.7 us -> 28 us
    all_to_all x1, waiting for transfers between devices: 29.3 us -> 1.81 us  [per_device(): lax.all_to_all(examples.reshape(feats, rows // feats, depth), 'feat', 0, 0)]
    ppermute x1, waiting for transfers between devices: 0.01 us -> 26.5 us  [per_device(): lax.ppermute(examples, 'feat', [(f, (f + line) % feats) for f in range(fe...]
    ppermute x10, starting transfers between devices: 27.2 us -> 15.7 us  [swap(): return lax.ppermute(piece, 'ex', swap_pairs)]
    pallas_call x0 -> x2, Pallas kernels: none -> 7.96 us  [half_tiles(): pl.pallas_call(functools.partial(half_kernel, final), in_specs=specs, out...]
    ppermute x8, waiting for transfers between devices: 40.4 us -> 46.7 us  [per_device(): lax.ppermute(piece, 'ex', first_pairs if step == 0 else later_pairs)]
    pallas_call x2, Pallas kernels: 23.7 us -> 20 us  [tiles(): pl.pallas_call(functools.partial(tiles_kernel, sizes, 0 if out is None el...]
  transfers between devices with their start and end apart: 24 -> 24, of which waited for: 11 -> 12; matrix products, arithmetic and copies ran while one was open for 3% -> 3% of each run, Pallas kernels for 9% -> 13%
where the time goes in v3:
time: 186 us
  waiting for transfers between devices  93.4 us (50%)
  starting transfers between devices  44.5 us (24%)
  Pallas kernels  28 us (15%)
  between operations  13.7 us (7%)
  other arithmetic  3.67 us (2%)
  local copies, waits for them, and re-layouts  2.47 us (1%)
    ppermute x8, waiting for transfers between devices, per_device(): lax.ppermute(piece, 'ex', first_pairs if step == 0 else later_pairs)  46.7 us
    ppermute x1, waiting for transfers between devices, per_device(): lax.ppermute(examples, 'feat', [(f, (f + line) % feats) for f in range(fe...  26.5 us
    pallas_call x2, Pallas kernels, tiles(): pl.pallas_call(functools.partial(tiles_kernel, sizes, 0 if out is None el...  20 us
    ppermute x10, starting transfers between devices, swap(): return lax.ppermute(piece, 'ex', swap_pairs)  15.7 us
    ppermute x2, starting transfers between devices, per_device(): wrapped = [lax.ppermute(piece, 'ex', wrap_pairs) for piece in held]  15.2 us
    ppermute x2, waiting for transfers between devices, per_device(): wrapped = [lax.ppermute(piece, 'ex', wrap_pairs) for piece in held]  13.9 us
    pallas_call x2, Pallas kernels, half_tiles(): pl.pallas_call(functools.partial(half_kernel, final), in_specs=specs, out...  7.96 us
    ppermute x8, starting transfers between devices, per_device(): lax.ppermute(piece, 'ex', first_pairs if step == 0 else later_pairs)  5.73 us
  transfers between devices with their start and end apart: 24, of which 12 were waited for; matrix products, arithmetic and copies ran while one was open for 3% of the time, Pallas kernels for 13%

profile of v3, /device:TPU:1, one launch (start us, length us, event | category | flops | bytes accessed | tf_op | source)
XLA Modules:
  0.0 185.7 jit_solution(5229280056258290054)
XLA Ops:
  7.3 3.8 %collective-permute-start = (bf16[512,1024]{1,0:T(8,128)(2,1)}, bf16[512,1024]{1,0:T(8,128)(2,1)S(1)}, u32[]{:S(2)}, u32[]{:S(2)}) collective-permute-start(bf16[512,1024]{1,0:T(8,128)(2,1)} %param.1), channel_id=1, source_target_pairs={{0,4},{1,5},{2,6},{3,7},{4,0},{5,1},{6,2},{7,3},{8,12},{9,13},{10,... | collective-permute-start | bytes 3145736 | tf_op jit(solution)/shard_map/ppermute | solution.py:212
  11.1 4.0 %all-to-all-start = ((bf16[8,64,1024]{2,1,0:T(8,128)(2,1)}), bf16[8,64,1024]{2,1,0:T(8,128)(2,1)S(1)}, u32[]{:S(2)}, u32[]{:S(2)}) async-start(bf16[8,64,1024]{2,1,0:T(8,128)(2,1)} %bitcast.27), calls=%async_computation | async-start | bytes 2097152 | tf_op jit(solution)/shard_map/all_to_all | solution.py:213
  15.2 26.5 %collective-permute-done = bf16[512,1024]{1,0:T(8,128)(2,1)S(1)} collective-permute-done((bf16[512,1024]{1,0:T(8,128)(2,1)}, bf16[512,1024]{1,0:T(8,128)(2,1)S(1)}, u32[]{:S(2)}, u32[]{:S(2)}) %collective-permute-start) | collective-permute-done | bytes 1048608 | tf_op jit(solution)/shard_map/ppermute | solution.py:212
  42.7 1.8 all-to-all-done
  44.5 2.3 %collective-permute-start.1 = (bf16[4,64,1024]{2,1,0:T(8,128)(2,1)S(1)}, bf16[4,64,1024]{2,1,0:T(8,128)(2,1)S(1)}, u32[]{:S(2)}, u32[]{:S(2)}) collective-permute-start(bf16[4,64,1024]{2,1,0:T(8,128)(2,1)S(1)} %get-tuple-element.16), channel_id=1, source_target_pairs={{0,8},{8,0},{16,24},{24,16},{32,40},{40,32},{48,56},{56,48},{64,72... | collective-permute-start | bytes 1572872 | tf_op jit(solution)/shard_map/ppermute | solution.py:209
  48.4 3.3 %collective-permute-start.2 = (bf16[4,128,1024]{2,1,0:T(8,128)(2,1)S(1)}, bf16[4,128,1024]{2,1,0:T(8,128)(2,1)}, u32[]{:S(2)}, u32[]{:S(2)}) collective-permute-start(bf16[4,128,1024]{2,1,0:T(8,128)(2,1)S(1)} %pad_maximum_fusion.refs_2_), channel_id=1, source_target_pairs={{16,0},{32,16},{48,32},{64,48},{80,64},{96,80},{112,96},{144,128},... | collective-permute-start | bytes 3145736 | tf_op jit(solution)/shard_map/ppermute | solution.py:238
  51.8 2.0 %collective-permute-start.8 = (bf16[4,128,1024]{2,1,0:T(8,128)(2,1)S(1)}, bf16[4,128,1024]{2,1,0:T(8,128)(2,1)}, u32[]{:S(2)}, u32[]{:S(2)}) collective-permute-start(bf16[4,128,1024]{2,1,0:T(8,128)(2,1)S(1)} %pad_maximum_fusion.1.refs_3_), channel_id=1, source_target_pairs={{16,0},{32,16},{48,32},{64,48},{80,64},{96,80},{112,96},{144,128},... | collective-permute-start | bytes 3145736 | tf_op jit(solution)/shard_map/ppermute | solution.py:238
  53.8 10.5 %collective-permute-done.2 = bf16[4,128,1024]{2,1,0:T(8,128)(2,1)} collective-permute-done((bf16[4,128,1024]{2,1,0:T(8,128)(2,1)S(1)}, bf16[4,128,1024]{2,1,0:T(8,128)(2,1)}, u32[]{:S(2)}, u32[]{:S(2)}) %collective-permute-start.2) | collective-permute-done | bytes 1048608 | tf_op jit(solution)/shard_map/ppermute | solution.py:238
  64.4 7.1 %collective-permute-start.3 = (bf16[4,128,1024]{2,1,0:T(8,128)(2,1)}, bf16[4,128,1024]{2,1,0:T(8,128)(2,1)S(1)}, u32[]{:S(2)}, u32[]{:S(2)}) collective-permute-start(bf16[4,128,1024]{2,1,0:T(8,128)(2,1)} %collective-permute-done.2), channel_id=1, source_target_pairs={{8,112},{136,240},{9,113},{137,241},{10,114},{138,242},{11,115},{1... | collective-permute-start | bytes 3145736 | tf_op jit(solution)/shard_map/ppermute | solution.py:240
  71.5 4.1 %collective-permute-done.8 = bf16[4,128,1024]{2,1,0:T(8,128)(2,1)} collective-permute-done((bf16[4,128,1024]{2,1,0:T(8,128)(2,1)S(1)}, bf16[4,128,1024]{2,1,0:T(8,128)(2,1)}, u32[]{:S(2)}, u32[]{:S(2)}) %collective-permute-start.8) | collective-permute-done | bytes 1048608 | tf_op jit(solution)/shard_map/ppermute | solution.py:238
  75.6 8.1 %collective-permute-start.9 = (bf16[4,128,1024]{2,1,0:T(8,128)(2,1)}, bf16[4,128,1024]{2,1,0:T(8,128)(2,1)}, u32[]{:S(2)}, u32[]{:S(2)}) collective-permute-start(bf16[4,128,1024]{2,1,0:T(8,128)(2,1)} %collective-permute-done.8), channel_id=1, source_target_pairs={{8,112},{136,240},{9,113},{137,241},{10,114},{138,242},{11,115},{1... | collective-permute-start | bytes 3145736 | tf_op jit(solution)/shard_map/ppermute | solution.py:240
  83.8 1.7 maximum_select_fusion.refs_4_
  85.5 13.9 %collective-permute-done.9 = bf16[4,128,1024]{2,1,0:T(8,128)(2,1)} collective-permute-done((bf16[4,128,1024]{2,1,0:T(8,128)(2,1)}, bf16[4,128,1024]{2,1,0:T(8,128)(2,1)}, u32[]{:S(2)}, u32[]{:S(2)}) %collective-permute-start.9) | collective-permute-done | bytes 1048608 | tf_op jit(solution)/shard_map/ppermute | solution.py:240
  102.6 5.0 %collective-permute-start.14 = (bf16[4,128,1024]{2,1,0:T(8,128)(2,1)S(1)}, bf16[4,128,1024]{2,1,0:T(8,128)(2,1)}, u32[]{:S(2)}, u32[]{:S(2)}) collective-permute-start(bf16[4,128,1024]{2,1,0:T(8,128)(2,1)S(1)} %maximum_select_fusion.refs_4_), channel_id=1, source_target_pairs={{0,8},{8,0},{16,24},{24,16},{32,40},{40,32},{48,56},{56,48},{64,72... | collective-permute-start | bytes 3145736 | tf_op jit(solution)/shard_map/ppermute | solution.py:209
  108.0 10.4 %collective-permute-done.10.refs_9_ = bf16[4,128,1024]{2,1,0:T(8,128)(2,1)} collective-permute-done((bf16[4,128,1024]{2,1,0:T(8,128)(2,1)S(1)}, bf16[4,128,1024]{2,1,0:T(8,128)(2,1)}, u32[]{:S(2)}, u32[]{:S(2)}) %collective-permute-start.10) | collective-permute-done | bytes 1048608 | tf_op jit(solution)/shard_map/ppermute | solution.py:238
  120.3 2.2 %collective-permute-done.17.refs_11_ = bf16[4,128,1024]{2,1,0:T(8,128)(2,1)} collective-permute-done((bf16[4,128,1024]{2,1,0:T(8,128)(2,1)}, bf16[4,128,1024]{2,1,0:T(8,128)(2,1)}, u32[]{:S(2)}, u32[]{:S(2)}) %collective-permute-start.17) | collective-permute-done | bytes 1048608 | tf_op jit(solution)/shard_map/ppermute | solution.py:209
  122.5 12.8 %shard_map.17.refs_6_ = f32[17,64,512]{2,1,0:T(8,128)} custom-call(s32[10]{0:T(128)S(1)} %stack.82.place_ref, bf16[4,512,1024]{2,1,0:T(8,128)(2,1)} %bitcast.21, bf16[4,512,1024]{2,1,0:T(8,128)(2,1)} %bitcast.24, bf16[4,128,1024]{2,1,0:T(8,128)(2,1)S(1)} %pad_maximum_fusion.refs_2_, bf16[4,128,1024]{2,1,0:T(8,128)(2,1)} %copy-done, ...), custom_call_target="tpu_custom_call" | custom-call | flops 5368709120 | bytes 20185088 | tf_op jit(solution)/shard_map/pallas_call | solution.py:85
  136.8 5.0 %collective-permute-start.13 = (bf16[4,128,1024]{2,1,0:T(8,128)(2,1)}, bf16[4,128,1024]{2,1,0:T(8,128)(2,1)}, u32[]{:S(2)}, u32[]{:S(2)}) collective-permute-start(bf16[4,128,1024]{2,1,0:T(8,128)(2,1)} %collective-permute-done.11.refs_3_), channel_id=1, source_target_pairs={{0,8},{8,0},{16,24},{24,16},{32,40},{40,32},{48,56},{56,48},{64,72... | collective-permute-start | bytes 3145736 | tf_op jit(solution)/shard_map/ppermute | solution.py:209
  141.8 6.1 %collective-permute-done.5.refs_2_ = bf16[4,128,1024]{2,1,0:T(8,128)(2,1)S(1)} collective-permute-done((bf16[4,128,1024]{2,1,0:T(8,128)(2,1)}, bf16[4,128,1024]{2,1,0:T(8,128)(2,1)S(1)}, u32[]{:S(2)}, u32[]{:S(2)}) %collective-permute-start.5) | collective-permute-done | bytes 1048608 | tf_op jit(solution)/shard_map/ppermute | solution.py:238
  148.5 10.6 %collective-permute-done.19.refs_1_ = bf16[4,128,1024]{2,1,0:T(8,128)(2,1)S(1)} collective-permute-done((bf16[4,128,1024]{2,1,0:T(8,128)(2,1)}, bf16[4,128,1024]{2,1,0:T(8,128)(2,1)S(1)}, u32[]{:S(2)}, u32[]{:S(2)}) %collective-permute-start.19) | collective-permute-done | bytes 1048608 | tf_op jit(solution)/shard_map/ppermute | solution.py:238
  159.6 7.3 %shard_map.18.refs_5_ = f32[17,64,512]{2,1,0:T(8,128)} custom-call(s32[4]{0:T(128)S(1)} %pad_add_fusion.1.place_ref, bf16[4,512,1024]{2,1,0:T(8,128)(2,1)} %bitcast.22, bf16[4,512,1024]{2,1,0:T(8,128)(2,1)} %bitcast.25, bf16[4,128,1024]{2,1,0:T(8,128)(2,1)S(1)} %collective-permute-done.5.refs_2_, ...), custom_call_target="tpu_custom_call", output_to_operand_aliasing={{}: (7, {})} | custom-call | flops 2147483648 | bytes 13107200 | tf_op jit(solution)/shard_map/pallas_call | solution.py:85
  166.9 3.4 %collective-permute-done.6.refs_2_ = bf16[4,128,1024]{2,1,0:T(8,128)(2,1)S(1)} collective-permute-done((bf16[4,128,1024]{2,1,0:T(8,128)(2,1)S(1)}, bf16[4,128,1024]{2,1,0:T(8,128)(2,1)S(1)}, u32[]{:S(2)}, u32[]{:S(2)}) %collective-permute-start.6) | collective-permute-done | bytes 1048608 | tf_op jit(solution)/shard_map/ppermute | solution.py:238
  170.8 3.3 %shard_map.19.refs_4_ = f32[256,512]{1,0:T(8,128)S(1)} custom-call(bf16[4,512,1024]{2,1,0:T(8,128)(2,1)} %bitcast.26, bf16[4,128,1024]{2,1,0:T(8,128)(2,1)S(1)} %collective-permute-done.19.refs_1_, bf16[4,128,1024]{2,1,0:T(8,128)(2,1)} %collective-permute-done.20.refs_2_), custom_call_target="tpu_custom_call" | custom-call | flops 1073741824 | bytes 6815744 | tf_op jit(solution)/shard_map/pallas_call | solution.py:165
  174.2 4.6 %shard_map.20 = f32[17,64,512]{2,1,0:T(8,128)} custom-call(s32[4]{0:T(128)S(1)} %pad_add_fusion.refs_0_, bf16[4,512,1024]{2,1,0:T(8,128)(2,1)} %bitcast.23, bf16[4,128,1024]{2,1,0:T(8,128)(2,1)S(1)} %collective-permute-done.6.refs_2_, bf16[4,128,1024]{2,1,0:T(8,128)(2,1)} %collective-permute-done.18.refs_3_, ...), custom_call_target="tpu_custom_call", output_to_operand_aliasing={{}: (5, {})} | custom-call | flops 1073741824 | bytes 6815744 | tf_op jit(solution)/shard_map/pallas_call | solution.py:165
  (48 shorter events, 12.2 us)
Async XLA Ops:
  6.5 113.3 %all-gather.5.cloned.1.call-start = ((), (), s32[]{:S(2)}) async-start(), calls=%async_computation.1 | async-start | bytes 5242880 | tf_op jit(solution)/shard_map/all_gather | solution.py:211
  7.3 34.4 %collective-permute-start = (bf16[512,1024]{1,0:T(8,128)(2,1)}, bf16[512,1024]{1,0:T(8,128)(2,1)S(1)}, u32[]{:S(2)}, u32[]{:S(2)}) collective-permute-start(bf16[512,1024]{1,0:T(8,128)(2,1)} %param.1), channel_id=1, source_target_pairs={{0,4},{1,5},{2,6},{3,7},{4,0},{5,1},{6,2},{7,3},{8,12},{9,13},{10,... | collective-permute-start | bytes 3145736 | tf_op jit(solution)/shard_map/ppermute | solution.py:212
  11.1 33.4 %all-to-all-start = ((bf16[8,64,1024]{2,1,0:T(8,128)(2,1)}), bf16[8,64,1024]{2,1,0:T(8,128)(2,1)S(1)}, u32[]{:S(2)}, u32[]{:S(2)}) async-start(bf16[8,64,1024]{2,1,0:T(8,128)(2,1)} %bitcast.27), calls=%async_computation | async-start | bytes 2097152 | tf_op jit(solution)/shard_map/all_to_all | solution.py:213
  15.1 107.4 %all-gather.7.cloned.1.call-start = ((), (), s32[]{:S(2)}) async-start(), calls=%async_computation.2 | async-start | bytes 5242880 | tf_op jit(solution)/shard_map/all_gather | solution.py:245
  44.5 3.8 %collective-permute-start.1 = (bf16[4,64,1024]{2,1,0:T(8,128)(2,1)S(1)}, bf16[4,64,1024]{2,1,0:T(8,128)(2,1)S(1)}, u32[]{:S(2)}, u32[]{:S(2)}) collective-permute-start(bf16[4,64,1024]{2,1,0:T(8,128)(2,1)S(1)} %get-tuple-element.16), channel_id=1, source_target_pairs={{0,8},{8,0},{16,24},{24,16},{32,40},{40,32},{48,56},{56,48},{64,72... | collective-permute-start | bytes 1572872 | tf_op jit(solution)/shard_map/ppermute | solution.py:209
  46.8 4.9 %collective-permute-start.7 = (bf16[4,64,1024]{2,1,0:T(8,128)(2,1)S(1)}, bf16[4,64,1024]{2,1,0:T(8,128)(2,1)S(1)}, u32[]{:S(2)}, u32[]{:S(2)}) collective-permute-start(bf16[4,64,1024]{2,1,0:T(8,128)(2,1)S(1)} %get-tuple-element.15), channel_id=1, source_target_pairs={{0,8},{8,0},{16,24},{24,16},{32,40},{40,32},{48,56},{56,48},{64,72... | collective-permute-start | bytes 1572872 | tf_op jit(solution)/shard_map/ppermute | solution.py:209
  48.4 15.9 %collective-permute-start.2 = (bf16[4,128,1024]{2,1,0:T(8,128)(2,1)S(1)}, bf16[4,128,1024]{2,1,0:T(8,128)(2,1)}, u32[]{:S(2)}, u32[]{:S(2)}) collective-permute-start(bf16[4,128,1024]{2,1,0:T(8,128)(2,1)S(1)} %pad_maximum_fusion.refs_2_), channel_id=1, source_target_pairs={{16,0},{32,16},{48,32},{64,48},{80,64},{96,80},{112,96},{144,128},... | collective-permute-start | bytes 3145736 | tf_op jit(solution)/shard_map/ppermute | solution.py:238
  51.8 23.8 %collective-permute-start.8 = (bf16[4,128,1024]{2,1,0:T(8,128)(2,1)S(1)}, bf16[4,128,1024]{2,1,0:T(8,128)(2,1)}, u32[]{:S(2)}, u32[]{:S(2)}) collective-permute-start(bf16[4,128,1024]{2,1,0:T(8,128)(2,1)S(1)} %pad_maximum_fusion.1.refs_3_), channel_id=1, source_target_pairs={{16,0},{32,16},{48,32},{64,48},{80,64},{96,80},{112,96},{144,128},... | collective-permute-start | bytes 3145736 | tf_op jit(solution)/shard_map/ppermute | solution.py:238
  64.4 19.3 %collective-permute-start.3 = (bf16[4,128,1024]{2,1,0:T(8,128)(2,1)}, bf16[4,128,1024]{2,1,0:T(8,128)(2,1)S(1)}, u32[]{:S(2)}, u32[]{:S(2)}) collective-permute-start(bf16[4,128,1024]{2,1,0:T(8,128)(2,1)} %collective-permute-done.2), channel_id=1, source_target_pairs={{8,112},{136,240},{9,113},{137,241},{10,114},{138,242},{11,115},{1... | collective-permute-start | bytes 3145736 | tf_op jit(solution)/shard_map/ppermute | solution.py:240
  75.6 23.9 %collective-permute-start.9 = (bf16[4,128,1024]{2,1,0:T(8,128)(2,1)}, bf16[4,128,1024]{2,1,0:T(8,128)(2,1)}, u32[]{:S(2)}, u32[]{:S(2)}) collective-permute-start(bf16[4,128,1024]{2,1,0:T(8,128)(2,1)} %collective-permute-done.8), channel_id=1, source_target_pairs={{8,112},{136,240},{9,113},{137,241},{10,114},{138,242},{11,115},{1... | collective-permute-start | bytes 3145736 | tf_op jit(solution)/shard_map/ppermute | solution.py:240
  85.4 22.1 %collective-permute-start.4 = (bf16[4,128,1024]{2,1,0:T(8,128)(2,1)S(1)}, bf16[4,128,1024]{2,1,0:T(8,128)(2,1)}, u32[]{:S(2)}, u32[]{:S(2)}) collective-permute-start(bf16[4,128,1024]{2,1,0:T(8,128)(2,1)S(1)} %maximum_select_fusion.refs_4_), channel_id=1, source_target_pairs={{0,240},{8,24},{16,0},{24,40},{32,16},{40,56},{48,32},{56,72},{64,... | collective-permute-start | bytes 3145736 | tf_op jit(solution)/shard_map/ppermute | solution.py:238
  102.5 15.9 %collective-permute-start.10 = (bf16[4,128,1024]{2,1,0:T(8,128)(2,1)S(1)}, bf16[4,128,1024]{2,1,0:T(8,128)(2,1)}, u32[]{:S(2)}, u32[]{:S(2)}) collective-permute-start(bf16[4,128,1024]{2,1,0:T(8,128)(2,1)S(1)} %maximum_select_fusion.1.refs_5_), channel_id=1, source_target_pairs={{0,240},{8,24},{16,0},{24,40},{32,16},{40,56},{48,32},{56,72},{64,... | collective-permute-start | bytes 3145736 | tf_op jit(solution)/shard_map/ppermute | solution.py:238
  102.6 17.3 %collective-permute-start.14 = (bf16[4,128,1024]{2,1,0:T(8,128)(2,1)S(1)}, bf16[4,128,1024]{2,1,0:T(8,128)(2,1)}, u32[]{:S(2)}, u32[]{:S(2)}) collective-permute-start(bf16[4,128,1024]{2,1,0:T(8,128)(2,1)S(1)} %maximum_select_fusion.refs_4_), channel_id=1, source_target_pairs={{0,8},{8,0},{16,24},{24,16},{32,40},{40,32},{48,56},{56,48},{64,72... | collective-permute-start | bytes 3145736 | tf_op jit(solution)/shard_map/ppermute | solution.py:209
  107.5 12.7 %collective-permute-start.15 = (bf16[4,128,1024]{2,1,0:T(8,128)(2,1)S(1)}, bf16[4,128,1024]{2,1,0:T(8,128)(2,1)}, u32[]{:S(2)}, u32[]{:S(2)}) collective-permute-start(bf16[4,128,1024]{2,1,0:T(8,128)(2,1)S(1)} %maximum_select_fusion.1.refs_5_), channel_id=1, source_target_pairs={{0,8},{8,0},{16,24},{24,16},{32,40},{40,32},{48,56},{56,48},{64,72... | collective-permute-start | bytes 3145736 | tf_op jit(solution)/shard_map/ppermute | solution.py:209
  107.5 12.7 %collective-permute-start.16 = (bf16[4,128,1024]{2,1,0:T(8,128)(2,1)}, bf16[4,128,1024]{2,1,0:T(8,128)(2,1)}, u32[]{:S(2)}, u32[]{:S(2)}) collective-permute-start(bf16[4,128,1024]{2,1,0:T(8,128)(2,1)} %collective-permute-done.4.refs_8_), channel_id=1, source_target_pairs={{0,8},{8,0},{16,24},{24,16},{32,40},{40,32},{48,56},{56,48},{64,72... | collective-permute-start | bytes 3145736 | tf_op jit(solution)/shard_map/ppermute | solution.py:209
  118.4 4.1 %collective-permute-start.17 = (bf16[4,128,1024]{2,1,0:T(8,128)(2,1)}, bf16[4,128,1024]{2,1,0:T(8,128)(2,1)}, u32[]{:S(2)}, u32[]{:S(2)}) collective-permute-start(bf16[4,128,1024]{2,1,0:T(8,128)(2,1)} %collective-permute-done.10.refs_9_), channel_id=1, source_target_pairs={{0,8},{8,0},{16,24},{24,16},{32,40},{40,32},{48,56},{56,48},{64,72... | collective-permute-start | bytes 3145736 | tf_op jit(solution)/shard_map/ppermute | solution.py:209
  119.8 16.9 %collective-permute-start.11 = (bf16[4,128,1024]{2,1,0:T(8,128)(2,1)}, bf16[4,128,1024]{2,1,0:T(8,128)(2,1)}, u32[]{:S(2)}, u32[]{:S(2)}) collective-permute-start(bf16[4,128,1024]{2,1,0:T(8,128)(2,1)} %collective-permute-done.10.refs_9_), channel_id=1, source_target_pairs={{0,240},{8,24},{16,0},{24,40},{32,16},{40,56},{48,32},{56,72},{64,... | collective-permute-start | bytes 3145736 | tf_op jit(solution)/shard_map/ppermute | solution.py:238
  119.8 28.0 %collective-permute-start.5 = (bf16[4,128,1024]{2,1,0:T(8,128)(2,1)}, bf16[4,128,1024]{2,1,0:T(8,128)(2,1)S(1)}, u32[]{:S(2)}, u32[]{:S(2)}) collective-permute-start(bf16[4,128,1024]{2,1,0:T(8,128)(2,1)} %collective-permute-done.4.refs_8_), channel_id=1, source_target_pairs={{0,240},{8,24},{16,0},{24,40},{32,16},{40,56},{48,32},{56,72},{64,... | collective-permute-start | bytes 3145736 | tf_op jit(solution)/shard_map/ppermute | solution.py:238
  136.8 22.4 %collective-permute-start.19 = (bf16[4,128,1024]{2,1,0:T(8,128)(2,1)}, bf16[4,128,1024]{2,1,0:T(8,128)(2,1)S(1)}, u32[]{:S(2)}, u32[]{:S(2)}) collective-permute-start(bf16[4,128,1024]{2,1,0:T(8,128)(2,1)} %collective-permute-done.11.refs_3_), channel_id=1, source_target_pairs={{0,240},{8,24},{16,0},{24,40},{32,16},{40,56},{48,32},{56,72},{64,... | collective-permute-start | bytes 3145736 | tf_op jit(solution)/shard_map/ppermute | solution.py:238
  136.8 22.9 %collective-permute-start.13 = (bf16[4,128,1024]{2,1,0:T(8,128)(2,1)}, bf16[4,128,1024]{2,1,0:T(8,128)(2,1)}, u32[]{:S(2)}, u32[]{:S(2)}) collective-permute-start(bf16[4,128,1024]{2,1,0:T(8,128)(2,1)} %collective-permute-done.11.refs_3_), channel_id=1, source_target_pairs={{0,8},{8,0},{16,24},{24,16},{32,40},{40,32},{48,56},{56,48},{64,72... | collective-permute-start | bytes 3145736 | tf_op jit(solution)/shard_map/ppermute | solution.py:209
  147.9 11.8 %collective-permute-start.12 = (bf16[4,128,1024]{2,1,0:T(8,128)(2,1)S(1)}, bf16[4,128,1024]{2,1,0:T(8,128)(2,1)}, u32[]{:S(2)}, u32[]{:S(2)}) collective-permute-start(bf16[4,128,1024]{2,1,0:T(8,128)(2,1)S(1)} %collective-permute-done.5.refs_2_), channel_id=1, source_target_pairs={{0,8},{8,0},{16,24},{24,16},{32,40},{40,32},{48,56},{56,48},{64,72... | collective-permute-start | bytes 3145736 | tf_op jit(solution)/shard_map/ppermute | solution.py:209
  148.4 21.9 %collective-permute-start.6 = (bf16[4,128,1024]{2,1,0:T(8,128)(2,1)S(1)}, bf16[4,128,1024]{2,1,0:T(8,128)(2,1)S(1)}, u32[]{:S(2)}, u32[]{:S(2)}) collective-permute-start(bf16[4,128,1024]{2,1,0:T(8,128)(2,1)S(1)} %collective-permute-done.5.refs_2_), channel_id=1, source_target_pairs={{0,240},{8,24},{16,0},{24,40},{32,16},{40,56},{48,32},{56,72},{64,... | collective-permute-start | bytes 3145736 | tf_op jit(solution)/shard_map/ppermute | solution.py:238
  159.1 11.7 %collective-permute-start.20 = (bf16[4,128,1024]{2,1,0:T(8,128)(2,1)S(1)}, bf16[4,128,1024]{2,1,0:T(8,128)(2,1)}, u32[]{:S(2)}, u32[]{:S(2)}) collective-permute-start(bf16[4,128,1024]{2,1,0:T(8,128)(2,1)S(1)} %collective-permute-done.19.refs_1_), channel_id=1, source_target_pairs={{0,8},{8,0},{16,24},{24,16},{32,40},{40,32},{48,56},{56,48},{64,72... | collective-permute-start | bytes 3145736 | tf_op jit(solution)/shard_map/ppermute | solution.py:209
  170.4 3.8 %collective-permute-start.18 = (bf16[4,128,1024]{2,1,0:T(8,128)(2,1)S(1)}, bf16[4,128,1024]{2,1,0:T(8,128)(2,1)}, u32[]{:S(2)}, u32[]{:S(2)}) collective-permute-start(bf16[4,128,1024]{2,1,0:T(8,128)(2,1)S(1)} %collective-permute-done.6.refs_2_), channel_id=1, source_target_pairs={{0,8},{8,0},{16,24},{24,16},{32,40},{40,32},{48,56},{56,48},{64,72... | collective-permute-start | bytes 3145736 | tf_op jit(solution)/shard_map/ppermute | solution.py:209
  (4 other events, 71.8 us)
Sparse Core Ops, SparseCore 0:
  9.2 55.2 all-gather.4
  66.3 52.2 all-gather.6

commit v4 on v3

--- a/solution.py
+++ b/solution.py
@@ -229,8 +229,6 @@
     held = start
     groups = [[start]]
     for step in range(steps):
-        if step == 2:
-            held = [after(held[0], near), held[1]]
         if step == steps - 1:
             early = 2 + 4 * (steps - 2)
             out = tiles(place[:early], near, far, groups[:-1], shape)

time: 186 us -> 186 us (level)
  local copies, waits for them, and re-layouts: 2.47 us -> 5.66 us
    ppermute x2, waiting for transfers between devices: 13.9 us -> 11.2 us  [per_device(): wrapped = [lax.ppermute(piece, 'ex', wrap_pairs) for piece in held]]
    ppermute x8, waiting for transfers between devices: 46.7 us -> 49.4 us  [per_device(): lax.ppermute(piece, 'ex', first_pairs if step == 0 else later_pairs)]
    ppermute x10, starting transfers between devices: 15.7 us -> 13.5 us  [swap(): return lax.ppermute(piece, 'ex', swap_pairs)]
    unnamed x8 -> x16, local copies, waits for them, and re-layouts: 0.98 us -> 2.97 us
where the time goes in v4:
time: 186 us; the launch traced here: 185 us
  waiting for transfers between devices  92.6 us (50%)
  starting transfers between devices  43 us (23%)
  Pallas kernels  28 us (15%)
  between operations  13.7 us (7%)
  local copies, waits for them, and re-layouts  5.66 us (3%)
  other arithmetic  2.46 us (1%)
    ppermute x8, waiting for transfers between devices, per_device(): lax.ppermute(piece, 'ex', first_pairs if step == 0 else later_pairs)  49.4 us
    ppermute x1, waiting for transfers between devices, per_device(): lax.ppermute(examples, 'feat', [(f, (f + line) % feats) for f in range(fe...  26.5 us
    pallas_call x2, Pallas kernels, tiles(): pl.pallas_call(functools.partial(tiles_kernel, sizes, 0 if out is None el...  20 us
    ppermute x2, starting transfers between devices, per_device(): wrapped = [lax.ppermute(piece, 'ex', wrap_pairs) for piece in held]  16.2 us
    ppermute x10, starting transfers between devices, swap(): return lax.ppermute(piece, 'ex', swap_pairs)  13.5 us
    ppermute x2, waiting for transfers between devices, per_device(): wrapped = [lax.ppermute(piece, 'ex', wrap_pairs) for piece in held]  11.2 us
    pallas_call x2, Pallas kernels, half_tiles(): pl.pallas_call(functools.partial(half_kernel, final), in_specs=specs, out...  7.95 us
    ppermute x8, starting transfers between devices, per_device(): lax.ppermute(piece, 'ex', first_pairs if step == 0 else later_pairs)  5.46 us
  transfers between devices with their start and end apart: 24, of which 12 were waited for; matrix products, arithmetic and copies ran while one was open for 3% of the time, Pallas kernels for 13%

profile of v4, /device:TPU:1, one launch (start us, length us, event | category | flops | bytes accessed | tf_op | source)
XLA Modules:
  0.0 185.4 jit_solution(8092129758701556273)
XLA Ops:
  7.3 3.8 %collective-permute-start = (bf16[512,1024]{1,0:T(8,128)(2,1)}, bf16[512,1024]{1,0:T(8,128)(2,1)S(1)}, u32[]{:S(2)}, u32[]{:S(2)}) collective-permute-start(bf16[512,1024]{1,0:T(8,128)(2,1)} %param.1), channel_id=1, source_target_pairs={{0,4},{1,5},{2,6},{3,7},{4,0},{5,1},{6,2},{7,3},{8,12},{9,13},{10,... | collective-permute-start | bytes 3145736 | tf_op jit(solution)/shard_map/ppermute | solution.py:212
  11.1 4.0 %all-to-all-start = ((bf16[8,64,1024]{2,1,0:T(8,128)(2,1)}), bf16[8,64,1024]{2,1,0:T(8,128)(2,1)S(1)}, u32[]{:S(2)}, u32[]{:S(2)}) async-start(bf16[8,64,1024]{2,1,0:T(8,128)(2,1)} %bitcast.27), calls=%async_computation | async-start | bytes 2097152 | tf_op jit(solution)/shard_map/all_to_all | solution.py:213
  15.2 26.5 %collective-permute-done = bf16[512,1024]{1,0:T(8,128)(2,1)S(1)} collective-permute-done((bf16[512,1024]{1,0:T(8,128)(2,1)}, bf16[512,1024]{1,0:T(8,128)(2,1)S(1)}, u32[]{:S(2)}, u32[]{:S(2)}) %collective-permute-start) | collective-permute-done | bytes 1048608 | tf_op jit(solution)/shard_map/ppermute | solution.py:212
  42.7 1.8 all-to-all-done
  44.5 2.3 %collective-permute-start.1 = (bf16[4,64,1024]{2,1,0:T(8,128)(2,1)S(1)}, bf16[4,64,1024]{2,1,0:T(8,128)(2,1)S(1)}, u32[]{:S(2)}, u32[]{:S(2)}) collective-permute-start(bf16[4,64,1024]{2,1,0:T(8,128)(2,1)S(1)} %get-tuple-element.14), channel_id=1, source_target_pairs={{0,8},{8,0},{16,24},{24,16},{32,40},{40,32},{48,56},{56,48},{64,72... | collective-permute-start | bytes 1572872 | tf_op jit(solution)/shard_map/ppermute | solution.py:209
  48.4 3.3 %collective-permute-start.2 = (bf16[4,128,1024]{2,1,0:T(8,128)(2,1)S(1)}, bf16[4,128,1024]{2,1,0:T(8,128)(2,1)}, u32[]{:S(2)}, u32[]{:S(2)}) collective-permute-start(bf16[4,128,1024]{2,1,0:T(8,128)(2,1)S(1)} %pad_maximum_fusion.refs_2_), channel_id=1, source_target_pairs={{16,0},{32,16},{48,32},{64,48},{80,64},{96,80},{112,96},{144,128},... | collective-permute-start | bytes 3145736 | tf_op jit(solution)/shard_map/ppermute | solution.py:236
  51.8 2.0 %collective-permute-start.8 = (bf16[4,128,1024]{2,1,0:T(8,128)(2,1)S(1)}, bf16[4,128,1024]{2,1,0:T(8,128)(2,1)S(1)}, u32[]{:S(2)}, u32[]{:S(2)}) collective-permute-start(bf16[4,128,1024]{2,1,0:T(8,128)(2,1)S(1)} %pad_maximum_fusion.1.refs_3_), channel_id=1, source_target_pairs={{16,0},{32,16},{48,32},{64,48},{80,64},{96,80},{112,96},{144,128},... | collective-permute-start | bytes 3145736 | tf_op jit(solution)/shard_map/ppermute | solution.py:236
  53.8 10.5 %collective-permute-done.2 = bf16[4,128,1024]{2,1,0:T(8,128)(2,1)} collective-permute-done((bf16[4,128,1024]{2,1,0:T(8,128)(2,1)S(1)}, bf16[4,128,1024]{2,1,0:T(8,128)(2,1)}, u32[]{:S(2)}, u32[]{:S(2)}) %collective-permute-start.2) | collective-permute-done | bytes 1048608 | tf_op jit(solution)/shard_map/ppermute | solution.py:236
  64.4 8.0 %collective-permute-start.3 = (bf16[4,128,1024]{2,1,0:T(8,128)(2,1)}, bf16[4,128,1024]{2,1,0:T(8,128)(2,1)}, u32[]{:S(2)}, u32[]{:S(2)}) collective-permute-start(bf16[4,128,1024]{2,1,0:T(8,128)(2,1)} %collective-permute-done.2), channel_id=1, source_target_pairs={{8,112},{136,240},{9,113},{137,241},{10,114},{138,242},{11,115},{1... | collective-permute-start | bytes 3145736 | tf_op jit(solution)/shard_map/ppermute | solution.py:238
  72.4 3.1 %collective-permute-done.8 = bf16[4,128,1024]{2,1,0:T(8,128)(2,1)S(1)} collective-permute-done((bf16[4,128,1024]{2,1,0:T(8,128)(2,1)S(1)}, bf16[4,128,1024]{2,1,0:T(8,128)(2,1)S(1)}, u32[]{:S(2)}, u32[]{:S(2)}) %collective-permute-start.8) | collective-permute-done | bytes 1048608 | tf_op jit(solution)/shard_map/ppermute | solution.py:236
  75.5 8.2 %collective-permute-start.9 = (bf16[4,128,1024]{2,1,0:T(8,128)(2,1)S(1)}, bf16[4,128,1024]{2,1,0:T(8,128)(2,1)}, u32[]{:S(2)}, u32[]{:S(2)}) collective-permute-start(bf16[4,128,1024]{2,1,0:T(8,128)(2,1)S(1)} %collective-permute-done.8), channel_id=1, source_target_pairs={{8,112},{136,240},{9,113},{137,241},{10,114},{138,242},{11,115},{1... | collective-permute-start | bytes 3145736 | tf_op jit(solution)/shard_map/ppermute | solution.py:238
  85.0 1.7 maximum_select_fusion.refs_4_
  86.8 11.2 %collective-permute-done.9 = bf16[4,128,1024]{2,1,0:T(8,128)(2,1)} collective-permute-done((bf16[4,128,1024]{2,1,0:T(8,128)(2,1)S(1)}, bf16[4,128,1024]{2,1,0:T(8,128)(2,1)}, u32[]{:S(2)}, u32[]{:S(2)}) %collective-permute-start.9) | collective-permute-done | bytes 1048608 | tf_op jit(solution)/shard_map/ppermute | solution.py:238
  99.9 6.3 %collective-permute-start.14 = (bf16[4,128,1024]{2,1,0:T(8,128)(2,1)S(1)}, bf16[4,128,1024]{2,1,0:T(8,128)(2,1)S(1)}, u32[]{:S(2)}, u32[]{:S(2)}) collective-permute-start(bf16[4,128,1024]{2,1,0:T(8,128)(2,1)S(1)} %maximum_select_fusion.refs_4_), channel_id=1, source_target_pairs={{0,8},{8,0},{16,24},{24,16},{32,40},{40,32},{48,56},{56,48},{64,72... | collective-permute-start | bytes 3145736 | tf_op jit(solution)/shard_map/ppermute | solution.py:209
  106.7 9.0 %collective-permute-done.10.refs_9_ = bf16[4,128,1024]{2,1,0:T(8,128)(2,1)} collective-permute-done((bf16[4,128,1024]{2,1,0:T(8,128)(2,1)S(1)}, bf16[4,128,1024]{2,1,0:T(8,128)(2,1)}, u32[]{:S(2)}, u32[]{:S(2)}) %collective-permute-start.10) | collective-permute-done | bytes 1048608 | tf_op jit(solution)/shard_map/ppermute | solution.py:236
  115.7 2.8 %collective-permute-start.17 = (bf16[4,128,1024]{2,1,0:T(8,128)(2,1)}, bf16[4,128,1024]{2,1,0:T(8,128)(2,1)}, u32[]{:S(2)}, u32[]{:S(2)}) collective-permute-start(bf16[4,128,1024]{2,1,0:T(8,128)(2,1)} %collective-permute-done.10.refs_9_), channel_id=1, source_target_pairs={{0,8},{8,0},{16,24},{24,16},{32,40},{40,32},{48,56},{56,48},{64,72... | collective-permute-start | bytes 3145736 | tf_op jit(solution)/shard_map/ppermute | solution.py:209
  119.6 1.5 collective-permute-done.17.refs_11_
  121.2 12.8 %shard_map.17.refs_6_ = f32[17,64,512]{2,1,0:T(8,128)} custom-call(s32[10]{0:T(128)S(1)} %stack.82.place_ref, bf16[4,512,1024]{2,1,0:T(8,128)(2,1)} %bitcast.21, bf16[4,512,1024]{2,1,0:T(8,128)(2,1)} %bitcast.24, bf16[4,128,1024]{2,1,0:T(8,128)(2,1)S(1)} %pad_maximum_fusion.refs_2_, bf16[4,128,1024]{2,1,0:T(8,128)(2,1)} %copy-done, ...), custom_call_target="tpu_custom_call" | custom-call | flops 5368709120 | bytes 20185088 | tf_op jit(solution)/shard_map/pallas_call | solution.py:85
  135.5 11.1 %collective-permute-done.5.refs_2_ = bf16[4,128,1024]{2,1,0:T(8,128)(2,1)S(1)} collective-permute-done((bf16[4,128,1024]{2,1,0:T(8,128)(2,1)}, bf16[4,128,1024]{2,1,0:T(8,128)(2,1)S(1)}, u32[]{:S(2)}, u32[]{:S(2)}) %collective-permute-start.5) | collective-permute-done | bytes 1048608 | tf_op jit(solution)/shard_map/ppermute | solution.py:236
  147.2 10.6 %collective-permute-done.19.refs_1_ = bf16[4,128,1024]{2,1,0:T(8,128)(2,1)S(1)} collective-permute-done((bf16[4,128,1024]{2,1,0:T(8,128)(2,1)}, bf16[4,128,1024]{2,1,0:T(8,128)(2,1)S(1)}, u32[]{:S(2)}, u32[]{:S(2)}) %collective-permute-start.19) | collective-permute-done | bytes 1048608 | tf_op jit(solution)/shard_map/ppermute | solution.py:236
  158.3 7.3 %shard_map.18.refs_5_ = f32[17,64,512]{2,1,0:T(8,128)} custom-call(s32[4]{0:T(128)S(1)} %pad_add_fusion.1.place_ref, bf16[4,512,1024]{2,1,0:T(8,128)(2,1)} %bitcast.22, bf16[4,512,1024]{2,1,0:T(8,128)(2,1)} %bitcast.25, bf16[4,128,1024]{2,1,0:T(8,128)(2,1)S(1)} %collective-permute-done.5.refs_2_, ...), custom_call_target="tpu_custom_call", output_to_operand_aliasing={{}: (7, {})} | custom-call | flops 2147483648 | bytes 13107200 | tf_op jit(solution)/shard_map/pallas_call | solution.py:85
  165.6 3.4 %collective-permute-done.6.refs_2_ = bf16[4,128,1024]{2,1,0:T(8,128)(2,1)S(1)} collective-permute-done((bf16[4,128,1024]{2,1,0:T(8,128)(2,1)S(1)}, bf16[4,128,1024]{2,1,0:T(8,128)(2,1)S(1)}, u32[]{:S(2)}, u32[]{:S(2)}) %collective-permute-start.6) | collective-permute-done | bytes 1048608 | tf_op jit(solution)/shard_map/ppermute | solution.py:236
  169.5 3.3 %shard_map.19.refs_4_ = f32[256,512]{1,0:T(8,128)S(1)} custom-call(bf16[4,512,1024]{2,1,0:T(8,128)(2,1)} %bitcast.26, bf16[4,128,1024]{2,1,0:T(8,128)(2,1)S(1)} %collective-permute-done.19.refs_1_, bf16[4,128,1024]{2,1,0:T(8,128)(2,1)} %collective-permute-done.20.refs_2_), custom_call_target="tpu_custom_call" | custom-call | flops 1073741824 | bytes 6815744 | tf_op jit(solution)/shard_map/pallas_call | solution.py:165
  173.9 4.6 %shard_map.20 = f32[17,64,512]{2,1,0:T(8,128)} custom-call(s32[4]{0:T(128)S(1)} %pad_add_fusion.refs_0_, bf16[4,512,1024]{2,1,0:T(8,128)(2,1)} %bitcast.23, bf16[4,128,1024]{2,1,0:T(8,128)(2,1)S(1)} %collective-permute-done.6.refs_2_, bf16[4,128,1024]{2,1,0:T(8,128)(2,1)} %copy-done.7, ...), custom_call_target="tpu_custom_call", output_to_operand_aliasing={{}: (5, {})} | custom-call | flops 1073741824 | bytes 6815744 | tf_op jit(solution)/shard_map/pallas_call | solution.py:165
  (56 shorter events, 12.5 us)
Async XLA Ops:
  6.5 114.6 %all-gather.5.cloned.1.call-start = ((), (), s32[]{:S(2)}) async-start(), calls=%async_computation.1 | async-start | bytes 5242880 | tf_op jit(solution)/shard_map/all_gather | solution.py:211
  7.3 34.4 %collective-permute-start = (bf16[512,1024]{1,0:T(8,128)(2,1)}, bf16[512,1024]{1,0:T(8,128)(2,1)S(1)}, u32[]{:S(2)}, u32[]{:S(2)}) collective-permute-start(bf16[512,1024]{1,0:T(8,128)(2,1)} %param.1), channel_id=1, source_target_pairs={{0,4},{1,5},{2,6},{3,7},{4,0},{5,1},{6,2},{7,3},{8,12},{9,13},{10,... | collective-permute-start | bytes 3145736 | tf_op jit(solution)/shard_map/ppermute | solution.py:212
  11.1 33.4 %all-to-all-start = ((bf16[8,64,1024]{2,1,0:T(8,128)(2,1)}), bf16[8,64,1024]{2,1,0:T(8,128)(2,1)S(1)}, u32[]{:S(2)}, u32[]{:S(2)}) async-start(bf16[8,64,1024]{2,1,0:T(8,128)(2,1)} %bitcast.27), calls=%async_computation | async-start | bytes 2097152 | tf_op jit(solution)/shard_map/all_to_all | solution.py:213
  15.1 106.1 %all-gather.7.cloned.1.call-start = ((), (), s32[]{:S(2)}) async-start(), calls=%async_computation.2 | async-start | bytes 5242880 | tf_op jit(solution)/shard_map/all_gather | solution.py:243
  44.5 3.8 %collective-permute-start.1 = (bf16[4,64,1024]{2,1,0:T(8,128)(2,1)S(1)}, bf16[4,64,1024]{2,1,0:T(8,128)(2,1)S(1)}, u32[]{:S(2)}, u32[]{:S(2)}) collective-permute-start(bf16[4,64,1024]{2,1,0:T(8,128)(2,1)S(1)} %get-tuple-element.14), channel_id=1, source_target_pairs={{0,8},{8,0},{16,24},{24,16},{32,40},{40,32},{48,56},{56,48},{64,72... | collective-permute-start | bytes 1572872 | tf_op jit(solution)/shard_map/ppermute | solution.py:209
  46.8 4.9 %collective-permute-start.7 = (bf16[4,64,1024]{2,1,0:T(8,128)(2,1)S(1)}, bf16[4,64,1024]{2,1,0:T(8,128)(2,1)S(1)}, u32[]{:S(2)}, u32[]{:S(2)}) collective-permute-start(bf16[4,64,1024]{2,1,0:T(8,128)(2,1)S(1)} %get-tuple-element.13), channel_id=1, source_target_pairs={{0,8},{8,0},{16,24},{24,16},{32,40},{40,32},{48,56},{56,48},{64,72... | collective-permute-start | bytes 1572872 | tf_op jit(solution)/shard_map/ppermute | solution.py:209
  48.4 15.9 %collective-permute-start.2 = (bf16[4,128,1024]{2,1,0:T(8,128)(2,1)S(1)}, bf16[4,128,1024]{2,1,0:T(8,128)(2,1)}, u32[]{:S(2)}, u32[]{:S(2)}) collective-permute-start(bf16[4,128,1024]{2,1,0:T(8,128)(2,1)S(1)} %pad_maximum_fusion.refs_2_), channel_id=1, source_target_pairs={{16,0},{32,16},{48,32},{64,48},{80,64},{96,80},{112,96},{144,128},... | collective-permute-start | bytes 3145736 | tf_op jit(solution)/shard_map/ppermute | solution.py:236
  51.8 23.7 %collective-permute-start.8 = (bf16[4,128,1024]{2,1,0:T(8,128)(2,1)S(1)}, bf16[4,128,1024]{2,1,0:T(8,128)(2,1)S(1)}, u32[]{:S(2)}, u32[]{:S(2)}) collective-permute-start(bf16[4,128,1024]{2,1,0:T(8,128)(2,1)S(1)} %pad_maximum_fusion.1.refs_3_), channel_id=1, source_target_pairs={{16,0},{32,16},{48,32},{64,48},{80,64},{96,80},{112,96},{144,128},... | collective-permute-start | bytes 3145736 | tf_op jit(solution)/shard_map/ppermute | solution.py:236
  64.4 19.3 %collective-permute-start.3 = (bf16[4,128,1024]{2,1,0:T(8,128)(2,1)}, bf16[4,128,1024]{2,1,0:T(8,128)(2,1)}, u32[]{:S(2)}, u32[]{:S(2)}) collective-permute-start(bf16[4,128,1024]{2,1,0:T(8,128)(2,1)} %collective-permute-done.2), channel_id=1, source_target_pairs={{8,112},{136,240},{9,113},{137,241},{10,114},{138,242},{11,115},{1... | collective-permute-start | bytes 3145736 | tf_op jit(solution)/shard_map/ppermute | solution.py:238
  75.5 22.5 %collective-permute-start.9 = (bf16[4,128,1024]{2,1,0:T(8,128)(2,1)S(1)}, bf16[4,128,1024]{2,1,0:T(8,128)(2,1)}, u32[]{:S(2)}, u32[]{:S(2)}) collective-permute-start(bf16[4,128,1024]{2,1,0:T(8,128)(2,1)S(1)} %collective-permute-done.8), channel_id=1, source_target_pairs={{8,112},{136,240},{9,113},{137,241},{10,114},{138,242},{11,115},{1... | collective-permute-start | bytes 3145736 | tf_op jit(solution)/shard_map/ppermute | solution.py:238
  86.7 19.5 %collective-permute-start.4 = (bf16[4,128,1024]{2,1,0:T(8,128)(2,1)S(1)}, bf16[4,128,1024]{2,1,0:T(8,128)(2,1)}, u32[]{:S(2)}, u32[]{:S(2)}) collective-permute-start(bf16[4,128,1024]{2,1,0:T(8,128)(2,1)S(1)} %maximum_select_fusion.refs_4_), channel_id=1, source_target_pairs={{0,240},{8,24},{16,0},{24,40},{32,16},{40,56},{48,32},{56,72},{64,... | collective-permute-start | bytes 3145736 | tf_op jit(solution)/shard_map/ppermute | solution.py:236
  99.8 15.9 %collective-permute-start.10 = (bf16[4,128,1024]{2,1,0:T(8,128)(2,1)S(1)}, bf16[4,128,1024]{2,1,0:T(8,128)(2,1)}, u32[]{:S(2)}, u32[]{:S(2)}) collective-permute-start(bf16[4,128,1024]{2,1,0:T(8,128)(2,1)S(1)} %maximum_select_fusion.1.refs_5_), channel_id=1, source_target_pairs={{0,240},{8,24},{16,0},{24,40},{32,16},{40,56},{48,32},{56,72},{64,... | collective-permute-start | bytes 3145736 | tf_op jit(solution)/shard_map/ppermute | solution.py:236
  99.9 18.6 %collective-permute-start.14 = (bf16[4,128,1024]{2,1,0:T(8,128)(2,1)S(1)}, bf16[4,128,1024]{2,1,0:T(8,128)(2,1)S(1)}, u32[]{:S(2)}, u32[]{:S(2)}) collective-permute-start(bf16[4,128,1024]{2,1,0:T(8,128)(2,1)S(1)} %maximum_select_fusion.refs_4_), channel_id=1, source_target_pairs={{0,8},{8,0},{16,24},{24,16},{32,40},{40,32},{48,56},{56,48},{64,72... | collective-permute-start | bytes 3145736 | tf_op jit(solution)/shard_map/ppermute | solution.py:209
  106.2 13.4 %collective-permute-start.15 = (bf16[4,128,1024]{2,1,0:T(8,128)(2,1)S(1)}, bf16[4,128,1024]{2,1,0:T(8,128)(2,1)}, u32[]{:S(2)}, u32[]{:S(2)}) collective-permute-start(bf16[4,128,1024]{2,1,0:T(8,128)(2,1)S(1)} %maximum_select_fusion.1.refs_5_), channel_id=1, source_target_pairs={{0,8},{8,0},{16,24},{24,16},{32,40},{40,32},{48,56},{56,48},{64,72... | collective-permute-start | bytes 3145736 | tf_op jit(solution)/shard_map/ppermute | solution.py:209
  106.2 13.4 %collective-permute-start.16 = (bf16[4,128,1024]{2,1,0:T(8,128)(2,1)}, bf16[4,128,1024]{2,1,0:T(8,128)(2,1)}, u32[]{:S(2)}, u32[]{:S(2)}) collective-permute-start(bf16[4,128,1024]{2,1,0:T(8,128)(2,1)} %collective-permute-done.4.refs_8_), channel_id=1, source_target_pairs={{0,8},{8,0},{16,24},{24,16},{32,40},{40,32},{48,56},{56,48},{64,72... | collective-permute-start | bytes 3145736 | tf_op jit(solution)/shard_map/ppermute | solution.py:209
  115.7 5.4 %collective-permute-start.17 = (bf16[4,128,1024]{2,1,0:T(8,128)(2,1)}, bf16[4,128,1024]{2,1,0:T(8,128)(2,1)}, u32[]{:S(2)}, u32[]{:S(2)}) collective-permute-start(bf16[4,128,1024]{2,1,0:T(8,128)(2,1)} %collective-permute-done.10.refs_9_), channel_id=1, source_target_pairs={{0,8},{8,0},{16,24},{24,16},{32,40},{40,32},{48,56},{56,48},{64,72... | collective-permute-start | bytes 3145736 | tf_op jit(solution)/shard_map/ppermute | solution.py:209
  118.5 16.9 %collective-permute-start.11 = (bf16[4,128,1024]{2,1,0:T(8,128)(2,1)}, bf16[4,128,1024]{2,1,0:T(8,128)(2,1)}, u32[]{:S(2)}, u32[]{:S(2)}) collective-permute-start(bf16[4,128,1024]{2,1,0:T(8,128)(2,1)} %collective-permute-done.10.refs_9_), channel_id=1, source_target_pairs={{0,240},{8,24},{16,0},{24,40},{32,16},{40,56},{48,32},{56,72},{64,... | collective-permute-start | bytes 3145736 | tf_op jit(solution)/shard_map/ppermute | solution.py:236
  119.5 27.1 %collective-permute-start.5 = (bf16[4,128,1024]{2,1,0:T(8,128)(2,1)}, bf16[4,128,1024]{2,1,0:T(8,128)(2,1)S(1)}, u32[]{:S(2)}, u32[]{:S(2)}) collective-permute-start(bf16[4,128,1024]{2,1,0:T(8,128)(2,1)} %collective-permute-done.4.refs_8_), channel_id=1, source_target_pairs={{0,240},{8,24},{16,0},{24,40},{32,16},{40,56},{48,32},{56,72},{64,... | collective-permute-start | bytes 3145736 | tf_op jit(solution)/shard_map/ppermute | solution.py:236
  135.5 22.4 %collective-permute-start.19 = (bf16[4,128,1024]{2,1,0:T(8,128)(2,1)}, bf16[4,128,1024]{2,1,0:T(8,128)(2,1)S(1)}, u32[]{:S(2)}, u32[]{:S(2)}) collective-permute-start(bf16[4,128,1024]{2,1,0:T(8,128)(2,1)} %collective-permute-done.11.refs_3_), channel_id=1, source_target_pairs={{0,240},{8,24},{16,0},{24,40},{32,16},{40,56},{48,32},{56,72},{64,... | collective-permute-start | bytes 3145736 | tf_op jit(solution)/shard_map/ppermute | solution.py:236
  146.6 11.8 %collective-permute-start.12 = (bf16[4,128,1024]{2,1,0:T(8,128)(2,1)S(1)}, bf16[4,128,1024]{2,1,0:T(8,128)(2,1)}, u32[]{:S(2)}, u32[]{:S(2)}) collective-permute-start(bf16[4,128,1024]{2,1,0:T(8,128)(2,1)S(1)} %collective-permute-done.5.refs_2_), channel_id=1, source_target_pairs={{0,8},{8,0},{16,24},{24,16},{32,40},{40,32},{48,56},{56,48},{64,72... | collective-permute-start | bytes 3145736 | tf_op jit(solution)/shard_map/ppermute | solution.py:209
  147.1 11.2 %collective-permute-start.13 = (bf16[4,128,1024]{2,1,0:T(8,128)(2,1)}, bf16[4,128,1024]{2,1,0:T(8,128)(2,1)}, u32[]{:S(2)}, u32[]{:S(2)}) collective-permute-start(bf16[4,128,1024]{2,1,0:T(8,128)(2,1)} %collective-permute-done.11.refs_3_), channel_id=1, source_target_pairs={{0,8},{8,0},{16,24},{24,16},{32,40},{40,32},{48,56},{56,48},{64,72... | collective-permute-start | bytes 3145736 | tf_op jit(solution)/shard_map/ppermute | solution.py:209
  147.1 21.9 %collective-permute-start.6 = (bf16[4,128,1024]{2,1,0:T(8,128)(2,1)S(1)}, bf16[4,128,1024]{2,1,0:T(8,128)(2,1)S(1)}, u32[]{:S(2)}, u32[]{:S(2)}) collective-permute-start(bf16[4,128,1024]{2,1,0:T(8,128)(2,1)S(1)} %collective-permute-done.5.refs_2_), channel_id=1, source_target_pairs={{0,240},{8,24},{16,0},{24,40},{32,16},{40,56},{48,32},{56,72},{64,... | collective-permute-start | bytes 3145736 | tf_op jit(solution)/shard_map/ppermute | solution.py:236
  157.8 11.7 %collective-permute-start.20 = (bf16[4,128,1024]{2,1,0:T(8,128)(2,1)S(1)}, bf16[4,128,1024]{2,1,0:T(8,128)(2,1)}, u32[]{:S(2)}, u32[]{:S(2)}) collective-permute-start(bf16[4,128,1024]{2,1,0:T(8,128)(2,1)S(1)} %collective-permute-done.19.refs_1_), channel_id=1, source_target_pairs={{0,8},{8,0},{16,24},{24,16},{32,40},{40,32},{48,56},{56,48},{64,72... | collective-permute-start | bytes 3145736 | tf_op jit(solution)/shard_map/ppermute | solution.py:209
  169.1 3.8 %collective-permute-start.18 = (bf16[4,128,1024]{2,1,0:T(8,128)(2,1)S(1)}, bf16[4,128,1024]{2,1,0:T(8,128)(2,1)S(1)}, u32[]{:S(2)}, u32[]{:S(2)}) collective-permute-start(bf16[4,128,1024]{2,1,0:T(8,128)(2,1)S(1)} %collective-permute-done.6.refs_2_), channel_id=1, source_target_pairs={{0,8},{8,0},{16,24},{24,16},{32,40},{40,32},{48,56},{56,48},{64,72... | collective-permute-start | bytes 3145736 | tf_op jit(solution)/shard_map/ppermute | solution.py:209
  (8 other events, 96.1 us)
Sparse Core Ops, SparseCore 0:
  9.2 55.2 all-gather.4
  66.3 52.2 all-gather.6
